TPU v7x, 512 devices: a whole 4x4x16 slice. The times are simulated.
512 devices in a mesh: grp: 32 (over z, core), own: 16 (over y, x).
Axes of the slice: x: 4, y: 4, z: 16, core: 2. Of those that a mesh axis runs over, the one named last changes fastest.
Arguments:
- multipoles: bfloat16 [289, 65536], P(None, ('grp', 'own')), may hold values from -6 to 6
- operators: bfloat16 [320, 289, 289], P('own'), may hold values from -0.02734375 to 0.02734375
- targets: int32 [98304, 1], P(('grp', 'own')), may hold values from 0 to 15; in each aligned block of 3072 rows (0 to 3071, 3072 to 6143, ...) at most 288 rows name the same one
- sources: int32 [98304], P(('grp', 'own')), may hold values from 0 to 47
- classes: int32 [98304], P(('grp', 'own')), may hold values from 0 to 319, as said below
- owners: int32 [32, 16], P('grp'), may hold values from 0 to 15, each once within a row
Outputs:
- local_exp: float32 [289, 65536], P(None, ('grp', 'own'))
Inputs may be any that keep to these rules, and one draw needn't show every extreme that they name: `targets`: in each group's 3072 pairs no target block is named by more than 288 pairs; some group has a target named by exactly 288. `classes`: pair i has a class from o * 20 to (o + 1) * 20 - 1, where o = (i // 192) % 16. `owners`: each row is a permutation of 0 to 16 - 1.
All inputs are finite; a program needn't handle non-finite values.
Results may differ from a plain program's by a relative error of at most 0.0003.
Values may be sent and summed in bfloat16 or wider, within the bound.
No kernel may reach another device: no remote copies, remote signals or barrier semaphores. Data moves between devices by JAX's collectives and lax.ppermute only.
A program may use at most 64 MiB of HBM per device.

v0:
```python
import jax
import jax.numpy as jnp
from jax import lax
from jax.sharding import PartitionSpec as P

step_pairs = 32


def extended(value, sides, width):
    for axis, dim in sides:
        count, length = (lax.axis_size(axis), value.shape[dim])
        up = [(i, (i + 1) % count) for i in range(count - 1)]
        down = [(j, i) for i, j in up]
        last = lax.slice_in_dim(value, length - width, length, axis=dim)
        leading = lax.slice_in_dim(value, 0, width, axis=dim)
        before = lax.ppermute(last, axis, up)
        after = lax.ppermute(leading, axis, down)
        value = jnp.concatenate([before, value, after], axis=dim)
    return value


def per_device(multipoles, operators, targets, sources, classes, owners):
    own_n = lax.axis_size("own")
    me = lax.axis_index("own")
    coeffs = multipoles.shape[0]
    width = multipoles.shape[1]
    held = operators.shape[0]
    members = lax.all_gather(multipoles, "own", axis=1, tiled=True)
    panel = extended(members, (("grp", 1),), own_n * width)
    slot = sources % 3 * own_n + sources // 3
    blocks = panel.reshape(coeffs, 3 * own_n, width)
    target = targets[:, 0]
    count_pairs = target.shape[0]
    dest = jnp.take(owners[0], target)
    local_class = classes - me * held
    offsets = jnp.arange(step_pairs, dtype=jnp.int32)

    def spread_step(partial_value, turn):
        index = turn * step_pairs + offsets
        src_idx = jnp.take(slot, index)
        cls_idx = jnp.take(local_class, index)
        mats = jnp.take(operators, cls_idx, axis=0)
        picked = jnp.take(blocks, src_idx, axis=1)
        contrib = jnp.einsum("nqp,pnb->nqb", mats, picked, preferred_element_type=jnp.float32)
        rows = contrib.reshape(step_pairs, coeffs * width)
        return (partial_value.at[jnp.take(dest, index)].add(rows), None)

    turns = count_pairs // step_pairs
    start = jnp.zeros((own_n, coeffs * width), jnp.float32)
    partial_value, unused = lax.scan(spread_step, start, jnp.arange(turns, dtype=jnp.int32))
    moved = lax.all_to_all(partial_value, "own", split_axis=0, concat_axis=0, tiled=True)
    return jnp.sum(moved, axis=0).reshape(coeffs, width)


def solution(mesh):
    placed = (
        P(None, ("grp", "own")),
        P("own", None, None),
        P(("grp", "own"), None),
        P(("grp", "own")),
        P(("grp", "own")),
        P("grp", None),
    )
    return jax.shard_map(
        per_device, mesh=mesh, in_specs=placed, out_specs=P(None, ("grp", "own")), check_vma=False
    )
```

profile of v0, /device:TPU:1, one launch (start us, length us, event | category | flops | bytes accessed | tf_op | source)
XLA Modules:
  0.0 349.2 jit_solution(12124758509095169568)
XLA Ops:
  7.3 66.5 %all-gather.2.cloned.1.call-done = bf16[289,2048]{1,0:T(8,128)(2,1)} async-done(((bf16[289,128]{1,0:T(8,128)(2,1)}), bf16[289,2048]{1,0:T(8,128)(2,1)}) %all-gather.2.cloned.1.call-update) | async-done | bytes 1183760 | tf_op jit(solution)/shard_map/all_gather | solution.py:28
  73.7 3.8 %collective-permute-start.1 = (bf16[289,2048]{1,0:T(8,128)(2,1)}, bf16[289,2048]{1,0:T(8,128)(2,1)S(1)}, u32[]{:S(2)}, u32[]{:S(2)}) collective-permute-start(bf16[289,2048]{1,0:T(8,128)(2,1)} %all-gather.2.cloned.1.call-done), channel_id=1, source_target_pairs={{16,0},{32,16},{48,32},{64,48},{80,64},{96,80},{112,96},{128,112},... | collective-permute-start | bytes 3551240 | tf_op jit(solution)/shard_map/ppermute | solution.py:17
  82.6 5.1 %compare_select_fusion.5 = (s32[192,1]{0,1:T(1,128)S(1)}, s32[192,1]{0,1:T(1,128)S(1)}) fusion(s32[]{:T(128)} %bitcast.9, s32[]{:T(128)} %bitcast.10, s32[]{:T(128)} %bitcast.11, s32[]{:T(128)} %bitcast.12, s32[]{:T(128)} %bitcast.13, s32[]{:T(128)} %bitcast.15, s32[]{:T(128)} %bitcast.14, s32[192,1]{0,1:T(1,128)} %param.12), kind=kLoop, calls=%fused_computation.41 | loop fusion | flops 2880 | bytes 2332 | tf_op jit(solution)/shard_map/jit(_take)/gather | solution.py:34
  88.4 5.6 %select_select_fusion = s32[192]{0:T(256)S(1)} fusion(pred[192]{0:T(512)(128)(4,1)S(1)} %get-tuple-element.96, pred[192]{0:T(512)(128)(4,1)S(1)} %get-tuple-element.95, pred[192]{0:T(512)(128)(4,1)S(1)} %get-tuple-element.94, pred[192]{0:T(512)(128)(4,1)S(1)} %get-tuple-element.97, pred[192]{0:T(512)(128)(4,1)S(1)} %get-tuple-element.93, ...), kind=kLoop, calls=%fused_computation.52 | loop fusion | flops 1920 | bytes 3492 | tf_op jit(solution)/shard_map/jit(_take)/select_n | solution.py:34
  102.2 198.5 %while.11 = (s32[]{:T(128)}, f32[16,36992]{1,0:T(8,128)}, s32[6]{0:T(128)S(1)}, s32[192]{0:T(256)S(1)}, s32[192]{0:T(256)S(1)}, /*index=5*/bf16[20,289,289]{2,1,...) while((s32[]{:T(128)}, f32[16,36992]{1,0:T(8,128)}, ...), condition=%wide.region_2.4_spmd.clone, body=%wide.region_0.3_spmd.clone.sunk | while | flops 689248384 | bytes 35105872 | solution.py:50
  108.8 6.9 %gather_fusion.3 = bf16[32,289,289]{2,1,0:T(8,128)(2,1)} fusion(bf16[20,289,289]{2,1,0:T(8,128)(2,1)} %get-tuple-element.222, s32[1024]{0:T(1024)S(1)} %pad_clamp_fusion.7), kind=kCustom, calls=%fused_computation.3.clone.clone.1 | custom fusion | bytes 10690816 | tf_op jit(solution)/shard_map/while/body/eval_jaxpr/jit(_take)/gather | solution.py:42
  115.7 8.1 %fusion.24 = f32[32,289,128]{2,1,0:T(8,128)} fusion(bf16[32,289,289]{2,1,0:T(8,128)(2,1)} %gather_fusion.3, pred[32]{0:T(512)(128)(4,1)S(1)} %get-tuple-element.194, bf16[32,289,128]{2,1,0:T(8,128)(2,1)S(1)} %gather_fusion.4, pred[32]{0:T(512)(128)(4,1)S(1)} %get-tuple-element.196), kind=kOutput, calls=%fused_computation.7.clone.1 | convolution fusion | flops 688060416 | bytes 12447872 | tf_op jit(solution)/shard_map/while/body/eval_jaxpr/nqp,pnb->nqb/dot_general | solution.py:44
  123.8 11.6 %scatter_custom_fusion.6 = f32[16,36992]{1,0:T(8,128)} fusion(f32[16,36992]{1,0:T(8,128)} %get-tuple-element.208, s32[32]{0:T(128)S(1)} %compare_select_fusion.17, f32[4,8,289,128]{3,2,1,0:T(8,128)} %bitcast.37), kind=kCustom, calls=%fused_computation.10.clone.1 | custom fusion | flops 1183744 | bytes 7217152 | tf_op jit(solution)/shard_map/while/body/eval_jaxpr/scatter-add | solution.py:46
  142.0 6.9 %gather_fusion.3 = bf16[32,289,289]{2,1,0:T(8,128)(2,1)} fusion(bf16[20,289,289]{2,1,0:T(8,128)(2,1)} %get-tuple-element.222, s32[1024]{0:T(1024)S(1)} %pad_clamp_fusion.7), kind=kCustom, calls=%fused_computation.3.clone.clone.1 | custom fusion | bytes 10690816 | tf_op jit(solution)/shard_map/while/body/eval_jaxpr/jit(_take)/gather | solution.py:42
  148.9 8.1 %fusion.24 = f32[32,289,128]{2,1,0:T(8,128)} fusion(bf16[32,289,289]{2,1,0:T(8,128)(2,1)} %gather_fusion.3, pred[32]{0:T(512)(128)(4,1)S(1)} %get-tuple-element.194, bf16[32,289,128]{2,1,0:T(8,128)(2,1)S(1)} %gather_fusion.4, pred[32]{0:T(512)(128)(4,1)S(1)} %get-tuple-element.196), kind=kOutput, calls=%fused_computation.7.clone.1 | convolution fusion | flops 688060416 | bytes 12447872 | tf_op jit(solution)/shard_map/while/body/eval_jaxpr/nqp,pnb->nqb/dot_general | solution.py:44
  157.0 11.4 %scatter_custom_fusion.6 = f32[16,36992]{1,0:T(8,128)} fusion(f32[16,36992]{1,0:T(8,128)} %get-tuple-element.208, s32[32]{0:T(128)S(1)} %compare_select_fusion.17, f32[4,8,289,128]{3,2,1,0:T(8,128)} %bitcast.37), kind=kCustom, calls=%fused_computation.10.clone.1 | custom fusion | flops 1183744 | bytes 7217152 | tf_op jit(solution)/shard_map/while/body/eval_jaxpr/scatter-add | solution.py:46
  175.1 6.9 %gather_fusion.3 = bf16[32,289,289]{2,1,0:T(8,128)(2,1)} fusion(bf16[20,289,289]{2,1,0:T(8,128)(2,1)} %get-tuple-element.222, s32[1024]{0:T(1024)S(1)} %pad_clamp_fusion.7), kind=kCustom, calls=%fused_computation.3.clone.clone.1 | custom fusion | bytes 10690816 | tf_op jit(solution)/shard_map/while/body/eval_jaxpr/jit(_take)/gather | solution.py:42
  182.0 8.1 %fusion.24 = f32[32,289,128]{2,1,0:T(8,128)} fusion(bf16[32,289,289]{2,1,0:T(8,128)(2,1)} %gather_fusion.3, pred[32]{0:T(512)(128)(4,1)S(1)} %get-tuple-element.194, bf16[32,289,128]{2,1,0:T(8,128)(2,1)S(1)} %gather_fusion.4, pred[32]{0:T(512)(128)(4,1)S(1)} %get-tuple-element.196), kind=kOutput, calls=%fused_computation.7.clone.1 | convolution fusion | flops 688060416 | bytes 12447872 | tf_op jit(solution)/shard_map/while/body/eval_jaxpr/nqp,pnb->nqb/dot_general | solution.py:44
  190.1 11.4 %scatter_custom_fusion.6 = f32[16,36992]{1,0:T(8,128)} fusion(f32[16,36992]{1,0:T(8,128)} %get-tuple-element.208, s32[32]{0:T(128)S(1)} %compare_select_fusion.17, f32[4,8,289,128]{3,2,1,0:T(8,128)} %bitcast.37), kind=kCustom, calls=%fused_computation.10.clone.1 | custom fusion | flops 1183744 | bytes 7217152 | tf_op jit(solution)/shard_map/while/body/eval_jaxpr/scatter-add | solution.py:46
  208.1 6.9 %gather_fusion.3 = bf16[32,289,289]{2,1,0:T(8,128)(2,1)} fusion(bf16[20,289,289]{2,1,0:T(8,128)(2,1)} %get-tuple-element.222, s32[1024]{0:T(1024)S(1)} %pad_clamp_fusion.7), kind=kCustom, calls=%fused_computation.3.clone.clone.1 | custom fusion | bytes 10690816 | tf_op jit(solution)/shard_map/while/body/eval_jaxpr/jit(_take)/gather | solution.py:42
  215.0 8.1 %fusion.24 = f32[32,289,128]{2,1,0:T(8,128)} fusion(bf16[32,289,289]{2,1,0:T(8,128)(2,1)} %gather_fusion.3, pred[32]{0:T(512)(128)(4,1)S(1)} %get-tuple-element.194, bf16[32,289,128]{2,1,0:T(8,128)(2,1)S(1)} %gather_fusion.4, pred[32]{0:T(512)(128)(4,1)S(1)} %get-tuple-element.196), kind=kOutput, calls=%fused_computation.7.clone.1 | convolution fusion | flops 688060416 | bytes 12447872 | tf_op jit(solution)/shard_map/while/body/eval_jaxpr/nqp,pnb->nqb/dot_general | solution.py:44
  223.1 11.4 %scatter_custom_fusion.6 = f32[16,36992]{1,0:T(8,128)} fusion(f32[16,36992]{1,0:T(8,128)} %get-tuple-element.208, s32[32]{0:T(128)S(1)} %compare_select_fusion.17, f32[4,8,289,128]{3,2,1,0:T(8,128)} %bitcast.37), kind=kCustom, calls=%fused_computation.10.clone.1 | custom fusion | flops 1183744 | bytes 7217152 | tf_op jit(solution)/shard_map/while/body/eval_jaxpr/scatter-add | solution.py:46
  241.2 6.9 %gather_fusion.3 = bf16[32,289,289]{2,1,0:T(8,128)(2,1)} fusion(bf16[20,289,289]{2,1,0:T(8,128)(2,1)} %get-tuple-element.222, s32[1024]{0:T(1024)S(1)} %pad_clamp_fusion.7), kind=kCustom, calls=%fused_computation.3.clone.clone.1 | custom fusion | bytes 10690816 | tf_op jit(solution)/shard_map/while/body/eval_jaxpr/jit(_take)/gather | solution.py:42
  248.1 8.1 %fusion.24 = f32[32,289,128]{2,1,0:T(8,128)} fusion(bf16[32,289,289]{2,1,0:T(8,128)(2,1)} %gather_fusion.3, pred[32]{0:T(512)(128)(4,1)S(1)} %get-tuple-element.194, bf16[32,289,128]{2,1,0:T(8,128)(2,1)S(1)} %gather_fusion.4, pred[32]{0:T(512)(128)(4,1)S(1)} %get-tuple-element.196), kind=kOutput, calls=%fused_computation.7.clone.1 | convolution fusion | flops 688060416 | bytes 12447872 | tf_op jit(solution)/shard_map/while/body/eval_jaxpr/nqp,pnb->nqb/dot_general | solution.py:44
  256.2 11.4 %scatter_custom_fusion.6 = f32[16,36992]{1,0:T(8,128)} fusion(f32[16,36992]{1,0:T(8,128)} %get-tuple-element.208, s32[32]{0:T(128)S(1)} %compare_select_fusion.17, f32[4,8,289,128]{3,2,1,0:T(8,128)} %bitcast.37), kind=kCustom, calls=%fused_computation.10.clone.1 | custom fusion | flops 1183744 | bytes 7217152 | tf_op jit(solution)/shard_map/while/body/eval_jaxpr/scatter-add | solution.py:46
  274.3 6.9 %gather_fusion.3 = bf16[32,289,289]{2,1,0:T(8,128)(2,1)} fusion(bf16[20,289,289]{2,1,0:T(8,128)(2,1)} %get-tuple-element.222, s32[1024]{0:T(1024)S(1)} %pad_clamp_fusion.7), kind=kCustom, calls=%fused_computation.3.clone.clone.1 | custom fusion | bytes 10690816 | tf_op jit(solution)/shard_map/while/body/eval_jaxpr/jit(_take)/gather | solution.py:42
  281.2 8.1 %fusion.24 = f32[32,289,128]{2,1,0:T(8,128)} fusion(bf16[32,289,289]{2,1,0:T(8,128)(2,1)} %gather_fusion.3, pred[32]{0:T(512)(128)(4,1)S(1)} %get-tuple-element.194, bf16[32,289,128]{2,1,0:T(8,128)(2,1)S(1)} %gather_fusion.4, pred[32]{0:T(512)(128)(4,1)S(1)} %get-tuple-element.196), kind=kOutput, calls=%fused_computation.7.clone.1 | convolution fusion | flops 688060416 | bytes 12447872 | tf_op jit(solution)/shard_map/while/body/eval_jaxpr/nqp,pnb->nqb/dot_general | solution.py:44
  289.3 11.4 %scatter_custom_fusion.6 = f32[16,36992]{1,0:T(8,128)} fusion(f32[16,36992]{1,0:T(8,128)} %get-tuple-element.208, s32[32]{0:T(128)S(1)} %compare_select_fusion.17, f32[4,8,289,128]{3,2,1,0:T(8,128)} %bitcast.37), kind=kCustom, calls=%fused_computation.10.clone.1 | custom fusion | flops 1183744 | bytes 7217152 | tf_op jit(solution)/shard_map/while/body/eval_jaxpr/scatter-add | solution.py:46
  304.0 36.0 %all_to_all.9 = f32[16,1,36992]{2,1,0:T(1,128)S(1)} all-to-all(f32[16,1,36992]{2,1,0:T(1,128)S(1)} %all_to_all.6), channel_id=1, replica_groups=mesh['grp'=32,'own'=16] {'own'}, dimensions={0} | all-to-all | bytes 4734976 | tf_op jit(solution)/shard_map/all_to_all | solution.py:51
  (82 shorter events, 55.7 us)
Async XLA Ops:
  6.5 67.2 %all-gather.2.cloned.1.call-start = ((), (), s32[]{:S(2)}) async-start(), calls=%async_computation.1 | async-start | bytes 1288192 | tf_op jit(solution)/shard_map/all_gather | solution.py:28
  73.7 20.3 %collective-permute-start.1 = (bf16[289,2048]{1,0:T(8,128)(2,1)}, bf16[289,2048]{1,0:T(8,128)(2,1)S(1)}, u32[]{:S(2)}, u32[]{:S(2)}) collective-permute-start(bf16[289,2048]{1,0:T(8,128)(2,1)} %all-gather.2.cloned.1.call-done), channel_id=1, source_target_pairs={{16,0},{32,16},{48,32},{64,48},{80,64},{96,80},{112,96},{128,112},... | collective-permute-start | bytes 3551240 | tf_op jit(solution)/shard_map/ppermute | solution.py:17
  77.5 16.9 %collective-permute-start = (bf16[289,2048]{1,0:T(8,128)(2,1)}, bf16[289,2048]{1,0:T(8,128)(2,1)S(1)}, u32[]{:S(2)}, u32[]{:S(2)}) collective-permute-start(bf16[289,2048]{1,0:T(8,128)(2,1)} %all-gather.2.cloned.1.call-done), channel_id=1, source_target_pairs={{0,16},{16,32},{32,48},{48,64},{64,80},{80,96},{96,112},{112,128},... | collective-permute-start | bytes 3551240 | tf_op jit(solution)/shard_map/ppermute | solution.py:16
Sparse Core Ops, SparseCore 0:
  10.3 63.3 all-gather.1
where the time goes:
time: 351 us; the launch traced here: 349 us
  local copies, waits for them, and re-layouts  87.5 us (25%)
  other arithmetic  84.8 us (24%)
  waiting for transfers between devices  67.6 us (19%)
  matrix products  48.6 us (14%)
  blocking collectives  36 us (10%)
  between operations  13.5 us (4%)
  starting transfers between devices  6.89 us (2%)
  loops' own time  4.45 us (1%)
    scatter-add x6, other arithmetic, spread_step(): return (partial_value.at[jnp.take(dest, index)].add(rows), None)  68.7 us
    all_gather x1, waiting for transfers between devices, per_device(): members = lax.all_gather(multipoles, 'own', axis=1, tiled=True)  66.5 us
    dot_general x6, matrix products, spread_step(): jnp.einsum('nqp,pnb->nqb', mats, picked, preferred_element_type=jnp.float32)  48.6 us
    gather x6, local copies, waits for them, and re-layouts, spread_step(): mats = jnp.take(operators, cls_idx, axis=0)  41.5 us
    all_to_all x1, blocking collectives, per_device(): lax.all_to_all(partial_value, 'own', split_axis=0, concat_axis=0, tiled=T...  36 us
    gather x6, local copies, waits for them, and re-layouts, spread_step(): picked = jnp.take(blocks, src_idx, axis=1)  18.3 us
  transfers between devices with their start and end apart: 3, of which 2 were waited for; matrix products, arithmetic and copies ran while one was open for 4% of the time, Pallas kernels for 0%

commit v1 on v0

v1 whole, which is shorter than its diff:
```python
import jax
import jax.numpy as jnp
from jax import lax
from jax.experimental import pallas as pl
from jax.experimental.pallas import tpu as pltpu
from jax.sharding import PartitionSpec as P

GROUP = 8
SLOTS = 256
VMEM = pl.BlockSpec(memory_space=pltpu.VMEM)
SMEM = pl.BlockSpec(memory_space=pltpu.SMEM)


def plan(target, sources, classes, owners, held):
    count = target.shape[0]
    own_n = owners.shape[0]
    odd = lax.rem(lax.axis_index("grp"), 2)
    shift = sources % 3
    kind = jnp.where(shift == 1, 0, jnp.where((shift == 0) == (odd == 0), 2, 1))
    local = classes - lax.axis_index("own") * held
    dest = jnp.sum(jnp.where(target[:, None] == jnp.arange(own_n)[None, :], owners[None, :], 0), axis=1)
    packed = local + 32 * (sources // 3) + 2048 * dest
    run = kind * held + local
    pos = jnp.arange(count)
    rank = jnp.sum((run[:, None] == run[None, :]) & (pos[None, :] < pos[:, None]), axis=1, dtype=jnp.int32)
    runs = jnp.arange(3 * held)
    length = jnp.sum(run[:, None] == runs[None, :], axis=0, dtype=jnp.int32)
    length = (length + 1) // 2 * 2
    offset = jnp.sum(jnp.where(runs[None, :] < run[:, None], length[None, :], 0), axis=1)
    slot = offset + rank
    empty = 2048 * own_n
    items = empty + jnp.sum(jnp.where(slot[None, :] == jnp.arange(SLOTS)[:, None], packed[None, :] - empty, 0), axis=1)
    ends = jnp.sum(jnp.where(runs[None, :] < held * jnp.arange(1, 4)[:, None], length[None, :], 0), axis=1) // 2
    return items.astype(jnp.int32), ends.astype(jnp.int32)


def add_items(items, first, last, operators, panel, total):
    coeffs = operators.shape[1]

    def one(i):
        left, right = items[2 * i], items[2 * i + 1]
        both = jnp.concatenate([panel[(left >> 5) & 63][:coeffs], panel[(right >> 5) & 63][:coeffs]], axis=1)
        made = jnp.dot(operators[left & 31], both, preferred_element_type=jnp.float32)
        return made, left >> 11, right >> 11

    def put(made, left, right):
        total[left, :coeffs] += made[:, :128]
        total[right, :coeffs] += made[:, 128:]

    def many(k, carry):
        for part in [one(first + k * GROUP + u) for u in range(GROUP)]:
            put(*part)
        return carry

    def single(i, carry):
        put(*one(i))
        return carry

    full = lax.div(last - first, GROUP)
    lax.fori_loop(0, full, many, 0)
    lax.fori_loop(first + full * GROUP, last, single, 0)


def near_kernel(items, ends, operators, own_panel, other_panel, total):
    total[...] = jnp.zeros_like(total)
    add_items(items, 0, ends[0], operators, own_panel, total)
    add_items(items, ends[0], ends[1], operators, other_panel, total)


def far_kernel(items, ends, operators, panel, begun, out, total):
    total[...] = begun[...]
    add_items(items, ends[1], ends[2], operators, panel, total)
    out[...] = total[: out.shape[0]]


def per_device(multipoles, operators, targets, sources, classes, owners):
    own_n = lax.axis_size("own")
    grp_n = lax.axis_size("grp")
    coeffs, width = multipoles.shape
    held = operators.shape[0]
    rows = (coeffs + 15) // 16 * 16
    sums = (coeffs + 7) // 8 * 8
    padded = jnp.pad(multipoles, ((0, rows - coeffs), (0, 0)))
    own_panel = lax.all_to_all(
        jnp.broadcast_to(padded, (own_n, rows, width)), "own", split_axis=0, concat_axis=0, tiled=True
    )
    across = [(i, i + 1) for i in range(1, grp_n - 1, 2)]
    far_panel = lax.ppermute(own_panel, "grp", across + [(j, i) for i, j in across])
    other_panel = lax.ppermute(own_panel, "grp", [(i, i ^ 1) for i in range(grp_n)])
    target, sources, classes, owner, unused = lax.optimization_barrier(
        (targets[:, 0], sources, classes, owners[0], own_panel)
    )
    items, ends = plan(target, sources, classes, owner, held)
    vmem = pltpu.CompilerParams(vmem_limit_bytes=32 * 2**20)
    pair = 2 * coeffs * coeffs * width
    begun = pl.pallas_call(
        near_kernel,
        out_shape=jax.ShapeDtypeStruct((own_n + 1, sums, width), jnp.float32),
        in_specs=[SMEM, SMEM, VMEM, VMEM, VMEM],
        out_specs=VMEM,
        compiler_params=vmem,
        cost_estimate=pl.CostEstimate(flops=3 * 128 * pair, bytes_accessed=2**23, transcendentals=0),
    )(items, ends, operators, own_panel, other_panel)
    partial = pl.pallas_call(
        far_kernel,
        out_shape=jax.ShapeDtypeStruct((own_n, sums, width), jnp.float32),
        in_specs=[SMEM, SMEM, VMEM, VMEM, VMEM],
        out_specs=VMEM,
        scratch_shapes=[pltpu.VMEM((own_n + 1, sums, width), jnp.float32)],
        compiler_params=vmem,
        cost_estimate=pl.CostEstimate(flops=3 * 64 * pair, bytes_accessed=2**23, transcendentals=0),
    )(items, ends, operators, far_panel, begun)
    moved = lax.all_to_all(partial, "own", split_axis=0, concat_axis=0, tiled=True)
    return jnp.sum(moved, axis=0)[:coeffs]


def solution(mesh):
    placed = (
        P(None, ("grp", "own")),
        P("own", None, None),
        P(("grp", "own"), None),
        P(("grp", "own")),
        P(("grp", "own")),
        P("grp", None),
    )
    return jax.shard_map(
        per_device, mesh=mesh, in_specs=placed, out_specs=P(None, ("grp", "own")), check_vma=False
    )
```

time: 351 us -> 94.8 us (0.27)
  the two profiles are of different devices: /device:TPU:1 before, /device:TPU:353 now
where the time goes in v1:
time: 94.8 us; the launch traced here: 94.5 us
  blocking collectives  36 us (38%)
  waiting for transfers between devices  22.2 us (23%)
  Pallas kernels  16.1 us (17%)
  starting transfers between devices  14.1 us (15%)
  local copies, waits for them, and re-layouts  4.43 us (5%)
  other arithmetic  1.63 us (2%)
    all_to_all x1, blocking collectives, per_device(): lax.all_to_all(partial, 'own', split_axis=0, concat_axis=0, tiled=True)  36 us
    all_to_all x1, waiting for transfers between devices, per_device(): lax.all_to_all(jnp.broadcast_to(padded, (own_n, rows, width)), 'own', spl...  18.1 us
    pallas_call x1, Pallas kernels, per_device(): pl.pallas_call(near_kernel, out_shape=jax.ShapeDtypeStruct((own_n + 1, su...  10.1 us
    all_to_all x1, starting transfers between devices, per_device(): lax.all_to_all(jnp.broadcast_to(padded, (own_n, rows, width)), 'own', spl...  6.75 us
    pallas_call x1, Pallas kernels, per_device(): pl.pallas_call(far_kernel, out_shape=jax.ShapeDtypeStruct((own_n, sums, w...  5.93 us
    ppermute x1, starting transfers between devices, per_device(): lax.ppermute(own_panel, 'grp', [(i, i ^ 1) for i in range(grp_n)])  4.78 us
    ppermute x1, waiting for transfers between devices, per_device(): lax.ppermute(own_panel, 'grp', across + [(j, i) for i, j in across])  4.11 us
    ppermute x1, starting transfers between devices, per_device(): lax.ppermute(own_panel, 'grp', across + [(j, i) for i, j in across])  2.54 us
  transfers between devices with their start and end apart: 3, of which 2 were waited for; matrix products, arithmetic and copies ran while one was open for 1% of the time, Pallas kernels for 11%

profile of v1, /device:TPU:353, one launch (start us, length us, event | category | flops | bytes accessed | tf_op | source)
XLA Modules:
  0.0 94.5 jit_solution(15774138535342788979)
XLA Ops:
  0.0 0.0 copy-start.3
  0.0 0.9 pad.4
  1.0 1.2 %broadcast_in_dim.77 = bf16[16,304,128]{2,1,0:T(8,128)(2,1)} broadcast(bf16[304,128]{1,0:T(8,128)(2,1)S(1)} %pad.4), dimensions={1,2} | broadcast | bytes 1323008 | tf_op jit(solution)/shard_map/broadcast_in_dim | solution.py:85
  2.2 6.8 %all-to-all-start = ((bf16[16,304,128]{2,1,0:T(8,128)(2,1)}), bf16[16,304,128]{2,1,0:T(8,128)(2,1)S(1)}, u32[]{:S(2)}, u32[]{:S(2)}) async-start(bf16[16,304,128]{2,1,0:T(8,128)(2,1)} %broadcast_in_dim.77), calls=%async_computation | async-start | bytes 2490368 | tf_op jit(solution)/shard_map/all_to_all | solution.py:84
  8.9 18.1 %all-to-all-done.own_panel = bf16[16,304,128]{2,1,0:T(8,128)(2,1)S(1)} async-done(((bf16[16,304,128]{2,1,0:T(8,128)(2,1)}), bf16[16,304,128]{2,1,0:T(8,128)(2,1)S(1)}, u32[]{:S(2)}, u32[]{:S(2)}) %all-to-all-start) | async-done | bytes 1245216 | tf_op jit(solution)/shard_map/all_to_all | solution.py:84
  27.0 0.0 copy-done.1
  27.0 0.0 copy-done.4
  27.0 0.1 select_reduce_fusion.2
  27.1 0.0 copy-done.2
  27.1 4.8 %collective-permute-start.1 = (bf16[16,304,128]{2,1,0:T(8,128)(2,1)S(1)}, bf16[16,304,128]{2,1,0:T(8,128)(2,1)S(1)}, u32[]{:S(2)}, u32[]{:S(2)}) collective-permute-start(bf16[16,304,128]{2,1,0:T(8,128)(2,1)S(1)} %all-to-all-done.own_panel), channel_id=1, source_target_pairs={{0,16},{16,0},{32,48},{48,32},{64,80},{80,64},{96,112},{112,96},{1... | collective-permute-start | bytes 3735560 | tf_op jit(solution)/shard_map/ppermute | solution.py:89
  31.9 0.1 convert_reduce_fusion.1
  32.1 0.1 select_reduce_fusion.1
  32.2 0.2 convert_reduce_fusion
  32.4 2.5 %collective-permute-start = (bf16[16,304,128]{2,1,0:T(8,128)(2,1)S(1)}, bf16[16,304,128]{2,1,0:T(8,128)(2,1)S(1)}, u32[]{:S(2)}, u32[]{:S(2)}) collective-permute-start(bf16[16,304,128]{2,1,0:T(8,128)(2,1)S(1)} %all-to-all-done.own_panel), channel_id=1, source_target_pairs={{16,32},{48,64},{80,96},{112,128},{144,160},{176,192},{208,224},{2... | collective-permute-start | bytes 3735560 | tf_op jit(solution)/shard_map/ppermute | solution.py:88
  34.9 0.1 select_reduce_fusion
  35.1 0.2 select_reduce_fusion.3
  35.3 0.0 collective-permute-done.1.other_panel
  35.3 0.0 copy-start
  35.3 2.3 %copy-done = bf16[20,289,289]{2,1,0:T(8,128)(2,1)S(1)} copy-done((bf16[20,289,289]{2,1,0:T(8,128)(2,1)S(1)}, bf16[20,289,289]{2,1,0:T(8,128)(2,1)}, u32[]{:S(2)}) %copy-start) | copy-done | bytes 3340864
  37.6 10.1 %shard_map.64.begun = f32[17,296,128]{2,1,0:T(8,128)S(1)} custom-call(s32[256]{0:T(256)S(1)} %broadcast_add_fusion.items, s32[3]{0:T(128)S(1)} %and_select_fusion.ends, bf16[20,289,289]{2,1,0:T(8,128)(2,1)S(1)} %copy-done, bf16[16,304,128]{2,1,0:T(8,128)(2,1)S(1)} %all-to-all-done.own_panel, bf16[16,304,128]{2,1,0:T(8,128)(2,1)S(1)} %collective-permute-done.1.other_panel), custom_call_target="tpu_custom_call" | custom-call | flops 8210448384 | bytes 8388608 | tf_op jit(solution)/shard_map/pallas_call | solution.py:96
  47.7 4.1 %collective-permute-done.panel = bf16[16,304,128]{2,1,0:T(8,128)(2,1)S(1)} collective-permute-done((bf16[16,304,128]{2,1,0:T(8,128)(2,1)S(1)}, bf16[16,304,128]{2,1,0:T(8,128)(2,1)S(1)}, u32[]{:S(2)}, u32[]{:S(2)}) %collective-permute-start) | collective-permute-done | bytes 1245216 | tf_op jit(solution)/shard_map/ppermute | solution.py:88
  51.8 5.9 %shard_map.65 = f32[16,296,128]{2,1,0:T(8,128)S(1)} custom-call(s32[256]{0:T(256)S(1)} %broadcast_add_fusion.items, s32[3]{0:T(128)S(1)} %and_select_fusion.ends, bf16[20,289,289]{2,1,0:T(8,128)(2,1)S(1)} %copy-done, bf16[16,304,128]{2,1,0:T(8,128)(2,1)S(1)} %collective-permute-done.panel, f32[17,296,128]{2,1,0:T(8,128)S(1)} %shard_map.64.begun), custom_call_target="tpu_custom_call" | custom-call | flops 4105224192 | bytes 8388608 | tf_op jit(solution)/shard_map/pallas_call | solution.py:104
  57.7 36.0 %all_to_all.10 = f32[16,296,128]{2,1,0:T(8,128)S(1)} all-to-all(f32[16,296,128]{2,1,0:T(8,128)S(1)} %shard_map.65), channel_id=1, replica_groups=mesh['grp'=32,'own'=16] {'own'}, dimensions={0} | all-to-all | bytes 4849664 | tf_op jit(solution)/shard_map/all_to_all | solution.py:113
  93.7 0.8 reduce_sum.69
  (10 shorter events, 0.1 us)
Async XLA Ops:
  0.0 27.0 %copy-start.1 = (s32[192,1]{0,1:T(1,128)S(1)}, s32[192,1]{0,1:T(1,128)}, u32[]{:S(2)}) copy-start(s32[192,1]{0,1:T(1,128)} %param.8) | copy-start | bytes 2308
  0.0 27.0 %copy-start.4 = (s32[1,16]{1,0:T(1,128)S(1)}, s32[1,16]{1,0:T(1,128)}, u32[]{:S(2)}) copy-start(s32[1,16]{1,0:T(1,128)} %param.11) | copy-start | bytes 196
  0.0 27.1 %copy-start.2 = (s32[192]{0:T(256)S(1)}, s32[192]{0:T(256)}, u32[]{:S(2)}) copy-start(s32[192]{0:T(256)} %param.10) | copy-start | bytes 2308
  0.0 27.1 %copy-start.3 = (s32[192]{0:T(256)S(1)}, s32[192]{0:T(256)}, u32[]{:S(2)}) copy-start(s32[192]{0:T(256)} %param.9) | copy-start | bytes 2308
  2.2 24.9 %all-to-all-start = ((bf16[16,304,128]{2,1,0:T(8,128)(2,1)}), bf16[16,304,128]{2,1,0:T(8,128)(2,1)S(1)}, u32[]{:S(2)}, u32[]{:S(2)}) async-start(bf16[16,304,128]{2,1,0:T(8,128)(2,1)} %broadcast_in_dim.77), calls=%async_computation | async-start | bytes 2490368 | tf_op jit(solution)/shard_map/all_to_all | solution.py:84
  27.1 8.1 %collective-permute-start.1 = (bf16[16,304,128]{2,1,0:T(8,128)(2,1)S(1)}, bf16[16,304,128]{2,1,0:T(8,128)(2,1)S(1)}, u32[]{:S(2)}, u32[]{:S(2)}) collective-permute-start(bf16[16,304,128]{2,1,0:T(8,128)(2,1)S(1)} %all-to-all-done.own_panel), channel_id=1, source_target_pairs={{0,16},{16,0},{32,48},{48,32},{64,80},{80,64},{96,112},{112,96},{1... | collective-permute-start | bytes 3735560 | tf_op jit(solution)/shard_map/ppermute | solution.py:89
  32.4 19.4 %collective-permute-start = (bf16[16,304,128]{2,1,0:T(8,128)(2,1)S(1)}, bf16[16,304,128]{2,1,0:T(8,128)(2,1)S(1)}, u32[]{:S(2)}, u32[]{:S(2)}) collective-permute-start(bf16[16,304,128]{2,1,0:T(8,128)(2,1)S(1)} %all-to-all-done.own_panel), channel_id=1, source_target_pairs={{16,32},{48,64},{80,96},{112,128},{144,160},{176,192},{208,224},{2... | collective-permute-start | bytes 3735560 | tf_op jit(solution)/shard_map/ppermute | solution.py:88
  35.3 2.3 %copy-start = (bf16[20,289,289]{2,1,0:T(8,128)(2,1)S(1)}, bf16[20,289,289]{2,1,0:T(8,128)(2,1)}, u32[]{:S(2)}) copy-start(bf16[20,289,289]{2,1,0:T(8,128)(2,1)} %operators.3) | copy-start | bytes 10022524

commit v2 on v1

--- a/solution.py
+++ b/solution.py
@@ -7,6 +7,8 @@
 
 GROUP = 8
 SLOTS = 256
+LEVELS = 32000.0
+FINE = 64.0
 VMEM = pl.BlockSpec(memory_space=pltpu.VMEM)
 SMEM = pl.BlockSpec(memory_space=pltpu.SMEM)
 
@@ -68,9 +70,30 @@
 
 
 def far_kernel(items, ends, operators, panel, begun, out, total):
+    coeffs = operators.shape[1]
     total[...] = begun[...]
     add_items(items, ends[1], ends[2], operators, panel, total)
-    out[...] = total[: out.shape[0]]
+
+    def code(t, carry):
+        values = total[t]
+        top = jnp.maximum(jnp.max(jnp.abs(values), axis=0, keepdims=True), 1e-37)
+        level = jnp.ceil(jnp.log2(top) * FINE)
+        steps = jnp.round(values * jnp.exp2(level * (-1.0 / FINE)) * LEVELS)
+        row = lax.broadcasted_iota(jnp.int32, values.shape, 0)
+        out[t] = jnp.where(row < coeffs, steps, level).astype(jnp.int32).astype(jnp.int16)
+        return carry
+
+    lax.fori_loop(0, out.shape[0], code, 0)
+
+
+def sum_kernel(moved, out):
+    coeffs = out.shape[0]
+    result = jnp.zeros(out.shape, jnp.float32)
+    for j in range(moved.shape[0]):
+        values = moved[j].astype(jnp.int32).astype(jnp.float32)
+        scale = jnp.exp2(values[coeffs : coeffs + 1] * (1.0 / FINE)) * (1.0 / LEVELS)
+        result = result + values[:coeffs] * scale
+    out[...] = result
 
 
 def per_device(multipoles, operators, targets, sources, classes, owners):
@@ -78,8 +101,7 @@
     grp_n = lax.axis_size("grp")
     coeffs, width = multipoles.shape
     held = operators.shape[0]
-    rows = (coeffs + 15) // 16 * 16
-    sums = (coeffs + 7) // 8 * 8
+    rows = (coeffs + 16) // 16 * 16
     padded = jnp.pad(multipoles, ((0, rows - coeffs), (0, 0)))
     own_panel = lax.all_to_all(
         jnp.broadcast_to(padded, (own_n, rows, width)), "own", split_axis=0, concat_axis=0, tiled=True
@@ -95,7 +117,7 @@
     pair = 2 * coeffs * coeffs * width
     begun = pl.pallas_call(
         near_kernel,
-        out_shape=jax.ShapeDtypeStruct((own_n + 1, sums, width), jnp.float32),
+        out_shape=jax.ShapeDtypeStruct((own_n + 1, rows, width), jnp.float32),
         in_specs=[SMEM, SMEM, VMEM, VMEM, VMEM],
         out_specs=VMEM,
         compiler_params=vmem,
@@ -103,15 +125,21 @@
     )(items, ends, operators, own_panel, other_panel)
     partial = pl.pallas_call(
         far_kernel,
-        out_shape=jax.ShapeDtypeStruct((own_n, sums, width), jnp.float32),
+        out_shape=jax.ShapeDtypeStruct((own_n, rows, width), jnp.int16),
         in_specs=[SMEM, SMEM, VMEM, VMEM, VMEM],
         out_specs=VMEM,
-        scratch_shapes=[pltpu.VMEM((own_n + 1, sums, width), jnp.float32)],
+        scratch_shapes=[pltpu.VMEM((own_n + 1, rows, width), jnp.float32)],
         compiler_params=vmem,
         cost_estimate=pl.CostEstimate(flops=3 * 64 * pair, bytes_accessed=2**23, transcendentals=0),
     )(items, ends, operators, far_panel, begun)
     moved = lax.all_to_all(partial, "own", split_axis=0, concat_axis=0, tiled=True)
-    return jnp.sum(moved, axis=0)[:coeffs]
+    return pl.pallas_call(
+        sum_kernel,
+        out_shape=jax.ShapeDtypeStruct((coeffs, width), jnp.float32),
+        in_specs=[VMEM],
+        out_specs=VMEM,
+        compiler_params=vmem,
+    )(moved)
 
 
 def solution(mesh):

time: 94.8 us -> 83.3 us (0.88)
  blocking collectives: 36 us -> 23.8 us
  Pallas kernels: 16.1 us -> 17.3 us
    all_to_all x1, blocking collectives: 36 us -> 23.8 us  [per_device(): lax.all_to_all(partial, 'own', split_axis=0, concat_axis=0, tiled=True)]
    pallas_call x2 -> x3, Pallas kernels: 16.1 us -> 17.3 us  [the longest x1 10.1 us: per_device(): pl.pallas_call(near_kernel, out_shape=jax.ShapeDtypeStruct((own_n + 1, ro...]
  transfers between devices with their start and end apart: 3 -> 3, of which waited for: 2 -> 2; matrix products, arithmetic and copies ran while one was open for 1% -> 1% of each run, Pallas kernels for 11% -> 12%
where the time goes in v2:
time: 83.3 us; the launch traced here: 82.9 us
  blocking collectives  23.8 us (29%)
  waiting for transfers between devices  22.2 us (27%)
  Pallas kernels  17.3 us (21%)
  starting transfers between devices  14.2 us (17%)
  local copies, waits for them, and re-layouts  4.39 us (5%)
  other arithmetic  0.85 us (1%)
    all_to_all x1, blocking collectives, per_device(): lax.all_to_all(partial, 'own', split_axis=0, concat_axis=0, tiled=True)  23.8 us
    all_to_all x1, waiting for transfers between devices, per_device(): lax.all_to_all(jnp.broadcast_to(padded, (own_n, rows, width)), 'own', spl...  18.1 us
    pallas_call x1, Pallas kernels, per_device(): pl.pallas_call(near_kernel, out_shape=jax.ShapeDtypeStruct((own_n + 1, ro...  10.1 us
    all_to_all x1, starting transfers between devices, per_device(): lax.all_to_all(jnp.broadcast_to(padded, (own_n, rows, width)), 'own', spl...  6.9 us
    pallas_call x1, Pallas kernels, per_device(): pl.pallas_call(far_kernel, out_shape=jax.ShapeDtypeStruct((own_n, rows, w...  6.26 us
    ppermute x1, starting transfers between devices, per_device(): lax.ppermute(own_panel, 'grp', [(i, i ^ 1) for i in range(grp_n)])  4.78 us
    ppermute x1, waiting for transfers between devices, per_device(): lax.ppermute(own_panel, 'grp', across + [(j, i) for i, j in across])  4.14 us
    ppermute x1, starting transfers between devices, per_device(): lax.ppermute(own_panel, 'grp', across + [(j, i) for i, j in across])  2.54 us
  transfers between devices with their start and end apart: 3, of which 2 were waited for; matrix products, arithmetic and copies ran while one was open for 1% of the time, Pallas kernels for 12%

profile of v2, /device:TPU:353, one launch (start us, length us, event | category | flops | bytes accessed | tf_op | source)
XLA Modules:
  0.0 82.9 jit_solution(18200345392012296338)
XLA Ops:
  0.0 0.9 %pad.4 = bf16[304,128]{1,0:T(8,128)(2,1)S(1)} pad(bf16[289,128]{1,0:T(8,128)(2,1)} %param.6, bf16[]{:T(256)} %constant.60.clone.1), padding=0_15x0_0 | pad | bytes 151810 | tf_op jit(solution)/shard_map/jit(_pad)/pad | solution.py:105
  0.9 1.2 %broadcast_in_dim.77 = bf16[16,304,128]{2,1,0:T(8,128)(2,1)} broadcast(bf16[304,128]{1,0:T(8,128)(2,1)S(1)} %pad.4), dimensions={1,2} | broadcast | bytes 1323008 | tf_op jit(solution)/shard_map/broadcast_in_dim | solution.py:107
  2.1 6.9 %all-to-all-start = ((bf16[16,304,128]{2,1,0:T(8,128)(2,1)}), bf16[16,304,128]{2,1,0:T(8,128)(2,1)S(1)}, u32[]{:S(2)}, u32[]{:S(2)}) async-start(bf16[16,304,128]{2,1,0:T(8,128)(2,1)} %broadcast_in_dim.77), calls=%async_computation | async-start | bytes 2490368 | tf_op jit(solution)/shard_map/all_to_all | solution.py:106
  9.0 18.1 %all-to-all-done.own_panel = bf16[16,304,128]{2,1,0:T(8,128)(2,1)S(1)} async-done(((bf16[16,304,128]{2,1,0:T(8,128)(2,1)}), bf16[16,304,128]{2,1,0:T(8,128)(2,1)S(1)}, u32[]{:S(2)}, u32[]{:S(2)}) %all-to-all-start) | async-done | bytes 1245216 | tf_op jit(solution)/shard_map/all_to_all | solution.py:106
  27.1 0.0 copy-done.1
  27.1 0.0 copy-done.4
  27.1 0.1 select_reduce_fusion.2
  27.2 0.0 copy-done.2
  27.2 0.0 copy-done.3
  27.2 4.8 %collective-permute-start.1 = (bf16[16,304,128]{2,1,0:T(8,128)(2,1)S(1)}, bf16[16,304,128]{2,1,0:T(8,128)(2,1)S(1)}, u32[]{:S(2)}, u32[]{:S(2)}) collective-permute-start(bf16[16,304,128]{2,1,0:T(8,128)(2,1)S(1)} %all-to-all-done.own_panel), channel_id=1, source_target_pairs={{0,16},{16,0},{32,48},{48,32},{64,80},{80,64},{96,112},{112,96},{1... | collective-permute-start | bytes 3735560 | tf_op jit(solution)/shard_map/ppermute | solution.py:111
  32.0 0.1 convert_reduce_fusion.1
  32.2 0.1 select_reduce_fusion.1
  32.3 0.2 convert_reduce_fusion
  32.5 2.5 %collective-permute-start = (bf16[16,304,128]{2,1,0:T(8,128)(2,1)S(1)}, bf16[16,304,128]{2,1,0:T(8,128)(2,1)S(1)}, u32[]{:S(2)}, u32[]{:S(2)}) collective-permute-start(bf16[16,304,128]{2,1,0:T(8,128)(2,1)S(1)} %all-to-all-done.own_panel), channel_id=1, source_target_pairs={{16,32},{48,64},{80,96},{112,128},{144,160},{176,192},{208,224},{2... | collective-permute-start | bytes 3735560 | tf_op jit(solution)/shard_map/ppermute | solution.py:110
  35.0 0.1 select_reduce_fusion
  35.1 0.2 select_reduce_fusion.3
  35.4 0.0 collective-permute-done.1.other_panel
  35.4 0.0 copy-start
  35.4 2.3 %copy-done = bf16[20,289,289]{2,1,0:T(8,128)(2,1)S(1)} copy-done((bf16[20,289,289]{2,1,0:T(8,128)(2,1)S(1)}, bf16[20,289,289]{2,1,0:T(8,128)(2,1)}, u32[]{:S(2)}) %copy-start) | copy-done | bytes 3340864
  37.7 10.1 %shard_map.64.begun = f32[17,304,128]{2,1,0:T(8,128)S(1)} custom-call(s32[256]{0:T(256)S(1)} %broadcast_add_fusion.items, s32[3]{0:T(128)S(1)} %and_select_fusion.ends, bf16[20,289,289]{2,1,0:T(8,128)(2,1)S(1)} %copy-done, bf16[16,304,128]{2,1,0:T(8,128)(2,1)S(1)} %all-to-all-done.own_panel, bf16[16,304,128]{2,1,0:T(8,128)(2,1)S(1)} %collective-permute-done.1.other_panel), custom_call_target="tpu_custom_call" | custom-call | flops 8210448384 | bytes 8388608 | tf_op jit(solution)/shard_map/pallas_call | solution.py:118
  47.8 4.1 %collective-permute-done.panel = bf16[16,304,128]{2,1,0:T(8,128)(2,1)S(1)} collective-permute-done((bf16[16,304,128]{2,1,0:T(8,128)(2,1)S(1)}, bf16[16,304,128]{2,1,0:T(8,128)(2,1)S(1)}, u32[]{:S(2)}, u32[]{:S(2)}) %collective-permute-start) | collective-permute-done | bytes 1245216 | tf_op jit(solution)/shard_map/ppermute | solution.py:110
  51.9 6.3 %shard_map.65 = s16[16,304,128]{2,1,0:T(8,128)(2,1)S(1)} custom-call(s32[256]{0:T(256)S(1)} %broadcast_add_fusion.items, s32[3]{0:T(128)S(1)} %and_select_fusion.ends, bf16[20,289,289]{2,1,0:T(8,128)(2,1)S(1)} %copy-done, bf16[16,304,128]{2,1,0:T(8,128)(2,1)S(1)} %collective-permute-done.panel, f32[17,304,128]{2,1,0:T(8,128)S(1)} %shard_map.64.begun), custom_call_target="tpu_custom_call" | custom-call | flops 4105224192 | bytes 8388608 | tf_op jit(solution)/shard_map/pallas_call | solution.py:126
  58.2 23.8 %all_to_all.10.moved = s16[16,304,128]{2,1,0:T(8,128)(2,1)S(1)} all-to-all(s16[16,304,128]{2,1,0:T(8,128)(2,1)S(1)} %shard_map.65), channel_id=1, replica_groups=mesh['grp'=32,'own'=16] {'own'}, dimensions={0} | all-to-all | bytes 2490368 | tf_op jit(solution)/shard_map/all_to_all | solution.py:135
  82.0 1.0 %shard_map.66 = f32[289,128]{1,0:T(8,128)} custom-call(s16[16,304,128]{2,1,0:T(8,128)(2,1)S(1)} %all_to_all.10.moved), custom_call_target="tpu_custom_call" | custom-call | tf_op jit(solution)/shard_map/pallas_call | solution.py:136
  (10 shorter events, 0.1 us)
Async XLA Ops:
  2.1 25.0 %copy-start.1 = (s32[192,1]{0,1:T(1,128)S(1)}, s32[192,1]{0,1:T(1,128)}, u32[]{:S(2)}) copy-start(s32[192,1]{0,1:T(1,128)} %param.8) | copy-start | bytes 2308
  2.1 25.0 %copy-start.4 = (s32[1,16]{1,0:T(1,128)S(1)}, s32[1,16]{1,0:T(1,128)}, u32[]{:S(2)}) copy-start(s32[1,16]{1,0:T(1,128)} %param.11) | copy-start | bytes 196
  2.1 25.1 %copy-start.2 = (s32[192]{0:T(256)S(1)}, s32[192]{0:T(256)}, u32[]{:S(2)}) copy-start(s32[192]{0:T(256)} %param.10) | copy-start | bytes 2308
  2.1 25.1 %copy-start.3 = (s32[192]{0:T(256)S(1)}, s32[192]{0:T(256)}, u32[]{:S(2)}) copy-start(s32[192]{0:T(256)} %param.9) | copy-start | bytes 2308
  2.1 25.0 %all-to-all-start = ((bf16[16,304,128]{2,1,0:T(8,128)(2,1)}), bf16[16,304,128]{2,1,0:T(8,128)(2,1)S(1)}, u32[]{:S(2)}, u32[]{:S(2)}) async-start(bf16[16,304,128]{2,1,0:T(8,128)(2,1)} %broadcast_in_dim.77), calls=%async_computation | async-start | bytes 2490368 | tf_op jit(solution)/shard_map/all_to_all | solution.py:106
  27.2 8.1 %collective-permute-start.1 = (bf16[16,304,128]{2,1,0:T(8,128)(2,1)S(1)}, bf16[16,304,128]{2,1,0:T(8,128)(2,1)S(1)}, u32[]{:S(2)}, u32[]{:S(2)}) collective-permute-start(bf16[16,304,128]{2,1,0:T(8,128)(2,1)S(1)} %all-to-all-done.own_panel), channel_id=1, source_target_pairs={{0,16},{16,0},{32,48},{48,32},{64,80},{80,64},{96,112},{112,96},{1... | collective-permute-start | bytes 3735560 | tf_op jit(solution)/shard_map/ppermute | solution.py:111
  32.5 19.4 %collective-permute-start = (bf16[16,304,128]{2,1,0:T(8,128)(2,1)S(1)}, bf16[16,304,128]{2,1,0:T(8,128)(2,1)S(1)}, u32[]{:S(2)}, u32[]{:S(2)}) collective-permute-start(bf16[16,304,128]{2,1,0:T(8,128)(2,1)S(1)} %all-to-all-done.own_panel), channel_id=1, source_target_pairs={{16,32},{48,64},{80,96},{112,128},{144,160},{176,192},{208,224},{2... | collective-permute-start | bytes 3735560 | tf_op jit(solution)/shard_map/ppermute | solution.py:110
  35.4 2.3 %copy-start = (bf16[20,289,289]{2,1,0:T(8,128)(2,1)S(1)}, bf16[20,289,289]{2,1,0:T(8,128)(2,1)}, u32[]{:S(2)}) copy-start(bf16[20,289,289]{2,1,0:T(8,128)(2,1)} %operators.3) | copy-start | bytes 10022524

commit v3 on v2

--- a/solution.py
+++ b/solution.py
@@ -1,3 +1,5 @@
+import math
+
 import jax
 import jax.numpy as jnp
 from jax import lax
@@ -5,9 +7,10 @@
 from jax.experimental.pallas import tpu as pltpu
 from jax.sharding import PartitionSpec as P
 
-GROUP = 8
+GROUPS = (16, 4, 1)
 SLOTS = 256
 LEVELS = 32000.0
+LEVEL_BITS = math.log2(LEVELS)
 FINE = 64.0
 VMEM = pl.BlockSpec(memory_space=pltpu.VMEM)
 SMEM = pl.BlockSpec(memory_space=pltpu.SMEM)
@@ -49,18 +52,25 @@
         total[left, :coeffs] += made[:, :128]
         total[right, :coeffs] += made[:, 128:]
 
-    def many(k, carry):
-        for part in [one(first + k * GROUP + u) for u in range(GROUP)]:
-            put(*part)
-        return carry
+    for size in GROUPS:
 
-    def single(i, carry):
-        put(*one(i))
-        return carry
+        def step(k, carry, first=first, size=size):
+            for part in [one(first + k * size + u) for u in range(size)]:
+                put(*part)
+            return carry
 
-    full = lax.div(last - first, GROUP)
-    lax.fori_loop(0, full, many, 0)
-    lax.fori_loop(first + full * GROUP, last, single, 0)
+        full = lax.div(last - first, size)
+        lax.fori_loop(0, full, step, 0)
+        first = first + full * size
+
+
+def spread_kernel(block, out):
+    coeffs = block.shape[0]
+    whole = coeffs // 16 * 16
+    last = jnp.concatenate([block[whole:], jnp.zeros((out.shape[1] - coeffs, block.shape[1]), block.dtype)], axis=0)
+    for t in range(out.shape[0]):
+        out[t, :whole] = block[:whole]
+        out[t, whole:] = last
 
 
 def near_kernel(items, ends, operators, own_panel, other_panel, total):
@@ -71,19 +81,25 @@
 
 def far_kernel(items, ends, operators, panel, begun, out, total):
     coeffs = operators.shape[1]
+    whole = coeffs // 16 * 16
     total[...] = begun[...]
     add_items(items, ends[1], ends[2], operators, panel, total)
 
-    def code(t, carry):
+    def code(t):
         values = total[t]
-        top = jnp.maximum(jnp.max(jnp.abs(values), axis=0, keepdims=True), 1e-37)
+        top = jnp.maximum(jnp.max(jnp.abs(values), axis=0, keepdims=True), 1e-32)
         level = jnp.ceil(jnp.log2(top) * FINE)
-        steps = jnp.round(values * jnp.exp2(level * (-1.0 / FINE)) * LEVELS)
-        row = lax.broadcasted_iota(jnp.int32, values.shape, 0)
-        out[t] = jnp.where(row < coeffs, steps, level).astype(jnp.int32).astype(jnp.int16)
+        steps = jnp.round(values * jnp.exp2(level * (-1.0 / FINE) + LEVEL_BITS))
+        row = lax.broadcasted_iota(jnp.int32, steps[whole:].shape, 0)
+        out[t, :whole] = steps[:whole].astype(jnp.int32).astype(jnp.int16)
+        out[t, whole:] = jnp.where(row < coeffs - whole, steps[whole:], level).astype(jnp.int32).astype(jnp.int16)
+
+    def some(k, carry):
+        for u in range(4):
+            code(4 * k + u)
         return carry
 
-    lax.fori_loop(0, out.shape[0], code, 0)
+    lax.fori_loop(0, out.shape[0] // 4, some, 0)
 
 
 def sum_kernel(moved, out):
@@ -102,17 +118,23 @@
     coeffs, width = multipoles.shape
     held = operators.shape[0]
     rows = (coeffs + 16) // 16 * 16
-    padded = jnp.pad(multipoles, ((0, rows - coeffs), (0, 0)))
+    spread = pl.pallas_call(
+        spread_kernel,
+        out_shape=jax.ShapeDtypeStruct((own_n, rows, width), multipoles.dtype),
+        in_specs=[VMEM],
+        out_specs=VMEM,
+        compiler_params=pltpu.CompilerParams(vmem_limit_bytes=8 * 2**20),
+    )(multipoles)
     own_panel = lax.all_to_all(
-        jnp.broadcast_to(padded, (own_n, rows, width)), "own", split_axis=0, concat_axis=0, tiled=True
+        spread, "own", split_axis=0, concat_axis=0, tiled=True
     )
     across = [(i, i + 1) for i in range(1, grp_n - 1, 2)]
     far_panel = lax.ppermute(own_panel, "grp", across + [(j, i) for i, j in across])
-    other_panel = lax.ppermute(own_panel, "grp", [(i, i ^ 1) for i in range(grp_n)])
     target, sources, classes, owner, unused = lax.optimization_barrier(
         (targets[:, 0], sources, classes, owners[0], own_panel)
     )
     items, ends = plan(target, sources, classes, owner, held)
+    other_panel = lax.ppermute(own_panel, "grp", [(i, i ^ 1) for i in range(grp_n)])
     vmem = pltpu.CompilerParams(vmem_limit_bytes=32 * 2**20)
     pair = 2 * coeffs * coeffs * width
     begun = pl.pallas_call(
@@ -121,7 +143,7 @@
         in_specs=[SMEM, SMEM, VMEM, VMEM, VMEM],
         out_specs=VMEM,
         compiler_params=vmem,
-        cost_estimate=pl.CostEstimate(flops=3 * 128 * pair, bytes_accessed=2**23, transcendentals=0),
+        cost_estimate=pl.CostEstimate(flops=pair, bytes_accessed=2**16, transcendentals=0),
     )(items, ends, operators, own_panel, other_panel)
     partial = pl.pallas_call(
         far_kernel,

time: 83.3 us -> 81.5 us (0.978)
  the two profiles are of different devices: /device:TPU:353 before, /device:TPU:96 now
where the time goes in v3:
time: 81.5 us; the launch traced here: 80.9 us
  blocking collectives  25.1 us (31%)
  waiting for transfers between devices  23 us (28%)
  Pallas kernels  17.3 us (21%)
  starting transfers between devices  11.2 us (14%)
  local copies, waits for them, and re-layouts  3.18 us (4%)
  other arithmetic  0.85 us (1%)
    all_to_all x1, blocking collectives, per_device(): lax.all_to_all(partial, 'own', split_axis=0, concat_axis=0, tiled=True)  25.1 us
    all_to_all x1, waiting for transfers between devices, per_device(): lax.all_to_all(spread, 'own', split_axis=0, concat_axis=0, tiled=True)  20 us
    pallas_call x1, Pallas kernels, per_device(): pl.pallas_call(near_kernel, out_shape=jax.ShapeDtypeStruct((own_n + 1, ro...  9.99 us
    all_to_all x1, starting transfers between devices, per_device(): lax.all_to_all(spread, 'own', split_axis=0, concat_axis=0, tiled=True)  7.18 us
    pallas_call x1, Pallas kernels, per_device(): pl.pallas_call(far_kernel, out_shape=jax.ShapeDtypeStruct((own_n, rows, w...  5.17 us
    unnamed x12, local copies, waits for them, and re-layouts  3.18 us
    ppermute x1, waiting for transfers between devices, per_device(): lax.ppermute(own_panel, 'grp', across + [(j, i) for i, j in across])  3.03 us
    ppermute x1, starting transfers between devices, per_device(): lax.ppermute(own_panel, 'grp', across + [(j, i) for i, j in across])  2.12 us
  transfers between devices with their start and end apart: 3, of which 2 were waited for; matrix products, arithmetic and copies ran while one was open for 1% of the time, Pallas kernels for 12%

profile of v3, /device:TPU:96, one launch (start us, length us, event | category | flops | bytes accessed | tf_op | source)
XLA Modules:
  0.0 80.9 jit_solution(1300247104014566255)
XLA Ops:
  0.0 0.9 %copy-done.1 = bf16[289,128]{1,0:T(8,128)(2,1)S(1)} copy-done((bf16[289,128]{1,0:T(8,128)(2,1)S(1)}, bf16[289,128]{1,0:T(8,128)(2,1)}, u32[]{:S(2)}) %copy-start.1) | copy-done | bytes 74008
  0.9 1.2 %shard_map.64 = bf16[16,304,128]{2,1,0:T(8,128)(2,1)} custom-call(bf16[289,128]{1,0:T(8,128)(2,1)S(1)} %copy-done.1), custom_call_target="tpu_custom_call" | custom-call | tf_op jit(solution)/shard_map/pallas_call | solution.py:121
  2.1 7.2 %all-to-all-start = ((bf16[16,304,128]{2,1,0:T(8,128)(2,1)}), bf16[16,304,128]{2,1,0:T(8,128)(2,1)S(1)}, u32[]{:S(2)}, u32[]{:S(2)}) async-start(bf16[16,304,128]{2,1,0:T(8,128)(2,1)} %shard_map.64), calls=%async_computation | async-start | bytes 2490368 | tf_op jit(solution)/shard_map/all_to_all | solution.py:128
  9.3 20.0 %all-to-all-done.own_panel = bf16[16,304,128]{2,1,0:T(8,128)(2,1)S(1)} async-done(((bf16[16,304,128]{2,1,0:T(8,128)(2,1)}), bf16[16,304,128]{2,1,0:T(8,128)(2,1)S(1)}, u32[]{:S(2)}, u32[]{:S(2)}) %all-to-all-start) | async-done | bytes 1245216 | tf_op jit(solution)/shard_map/all_to_all | solution.py:128
  29.3 0.0 copy-done.2
  29.3 0.0 copy-done.5
  29.3 0.1 select_reduce_fusion.2
  29.4 0.0 copy-done.3
  29.4 0.0 copy-done.4
  29.4 1.9 %collective-permute-start.1 = (bf16[16,304,128]{2,1,0:T(8,128)(2,1)S(1)}, bf16[16,304,128]{2,1,0:T(8,128)(2,1)S(1)}, u32[]{:S(2)}, u32[]{:S(2)}) collective-permute-start(bf16[16,304,128]{2,1,0:T(8,128)(2,1)S(1)} %all-to-all-done.own_panel), channel_id=1, source_target_pairs={{0,16},{16,0},{32,48},{48,32},{64,80},{80,64},{96,112},{112,96},{1... | collective-permute-start | bytes 3735560 | tf_op jit(solution)/shard_map/ppermute | solution.py:137
  31.4 2.1 %collective-permute-start = (bf16[16,304,128]{2,1,0:T(8,128)(2,1)S(1)}, bf16[16,304,128]{2,1,0:T(8,128)(2,1)S(1)}, u32[]{:S(2)}, u32[]{:S(2)}) collective-permute-start(bf16[16,304,128]{2,1,0:T(8,128)(2,1)S(1)} %all-to-all-done.own_panel), channel_id=1, source_target_pairs={{16,32},{48,64},{80,96},{112,128},{144,160},{176,192},{208,224},{2... | collective-permute-start | bytes 3735560 | tf_op jit(solution)/shard_map/ppermute | solution.py:132
  33.5 0.1 convert_reduce_fusion.1
  33.6 0.1 select_reduce_fusion.1
  33.7 0.2 convert_reduce_fusion
  33.9 0.2 select_reduce_fusion.3
  34.1 0.1 select_reduce_fusion
  34.3 0.0 collective-permute-done.1.other_panel
  34.3 0.0 copy-start
  34.3 2.3 %copy-done = bf16[20,289,289]{2,1,0:T(8,128)(2,1)S(1)} copy-done((bf16[20,289,289]{2,1,0:T(8,128)(2,1)S(1)}, bf16[20,289,289]{2,1,0:T(8,128)(2,1)}, u32[]{:S(2)}) %copy-start) | copy-done | bytes 3340864
  36.6 10.0 %shard_map.65.begun = f32[17,304,128]{2,1,0:T(8,128)S(1)} custom-call(s32[256]{0:T(256)S(1)} %broadcast_add_fusion.items, s32[3]{0:T(128)S(1)} %and_select_fusion.ends, bf16[20,289,289]{2,1,0:T(8,128)(2,1)S(1)} %copy-done, bf16[16,304,128]{2,1,0:T(8,128)(2,1)S(1)} %all-to-all-done.own_panel, bf16[16,304,128]{2,1,0:T(8,128)(2,1)S(1)} %collective-permute-done.1.other_panel), custom_call_target="tpu_custom_call" | custom-call | flops 21381376 | bytes 65536 | tf_op jit(solution)/shard_map/pallas_call | solution.py:140
  46.6 3.0 %collective-permute-done.panel = bf16[16,304,128]{2,1,0:T(8,128)(2,1)S(1)} collective-permute-done((bf16[16,304,128]{2,1,0:T(8,128)(2,1)S(1)}, bf16[16,304,128]{2,1,0:T(8,128)(2,1)S(1)}, u32[]{:S(2)}, u32[]{:S(2)}) %collective-permute-start) | collective-permute-done | bytes 1245216 | tf_op jit(solution)/shard_map/ppermute | solution.py:132
  49.6 5.2 %shard_map.66 = s16[16,304,128]{2,1,0:T(8,128)(2,1)S(1)} custom-call(s32[256]{0:T(256)S(1)} %broadcast_add_fusion.items, s32[3]{0:T(128)S(1)} %and_select_fusion.ends, bf16[20,289,289]{2,1,0:T(8,128)(2,1)S(1)} %copy-done, bf16[16,304,128]{2,1,0:T(8,128)(2,1)S(1)} %collective-permute-done.panel, f32[17,304,128]{2,1,0:T(8,128)S(1)} %shard_map.65.begun), custom_call_target="tpu_custom_call" | custom-call | flops 4105224192 | bytes 8388608 | tf_op jit(solution)/shard_map/pallas_call | solution.py:148
  54.8 25.1 %all_to_all.10.moved = s16[16,304,128]{2,1,0:T(8,128)(2,1)S(1)} all-to-all(s16[16,304,128]{2,1,0:T(8,128)(2,1)S(1)} %shard_map.66), channel_id=1, replica_groups=mesh['grp'=32,'own'=16] {'own'}, dimensions={0} | all-to-all | bytes 2490368 | tf_op jit(solution)/shard_map/all_to_all | solution.py:157
  79.9 1.0 %shard_map.67 = f32[289,128]{1,0:T(8,128)} custom-call(s16[16,304,128]{2,1,0:T(8,128)(2,1)S(1)} %all_to_all.10.moved), custom_call_target="tpu_custom_call" | custom-call | tf_op jit(solution)/shard_map/pallas_call | solution.py:158
  (11 shorter events, 0.1 us)
Async XLA Ops:
  0.0 0.9 %copy-start.1 = (bf16[289,128]{1,0:T(8,128)(2,1)S(1)}, bf16[289,128]{1,0:T(8,128)(2,1)}, u32[]{:S(2)}) copy-start(bf16[289,128]{1,0:T(8,128)(2,1)} %block.1) | copy-start | bytes 221956
  2.1 27.2 %copy-start.2 = (s32[192,1]{0,1:T(1,128)S(1)}, s32[192,1]{0,1:T(1,128)}, u32[]{:S(2)}) copy-start(s32[192,1]{0,1:T(1,128)} %param.8) | copy-start | bytes 2308
  2.1 27.2 %copy-start.5 = (s32[1,16]{1,0:T(1,128)S(1)}, s32[1,16]{1,0:T(1,128)}, u32[]{:S(2)}) copy-start(s32[1,16]{1,0:T(1,128)} %param.11) | copy-start | bytes 196
  2.1 27.3 %copy-start.3 = (s32[192]{0:T(256)S(1)}, s32[192]{0:T(256)}, u32[]{:S(2)}) copy-start(s32[192]{0:T(256)} %param.10) | copy-start | bytes 2308
  2.1 27.3 %copy-start.4 = (s32[192]{0:T(256)S(1)}, s32[192]{0:T(256)}, u32[]{:S(2)}) copy-start(s32[192]{0:T(256)} %param.9) | copy-start | bytes 2308
  2.1 27.2 %all-to-all-start = ((bf16[16,304,128]{2,1,0:T(8,128)(2,1)}), bf16[16,304,128]{2,1,0:T(8,128)(2,1)S(1)}, u32[]{:S(2)}, u32[]{:S(2)}) async-start(bf16[16,304,128]{2,1,0:T(8,128)(2,1)} %shard_map.64), calls=%async_computation | async-start | bytes 2490368 | tf_op jit(solution)/shard_map/all_to_all | solution.py:128
  29.4 4.8 %collective-permute-start.1 = (bf16[16,304,128]{2,1,0:T(8,128)(2,1)S(1)}, bf16[16,304,128]{2,1,0:T(8,128)(2,1)S(1)}, u32[]{:S(2)}, u32[]{:S(2)}) collective-permute-start(bf16[16,304,128]{2,1,0:T(8,128)(2,1)S(1)} %all-to-all-done.own_panel), channel_id=1, source_target_pairs={{0,16},{16,0},{32,48},{48,32},{64,80},{80,64},{96,112},{112,96},{1... | collective-permute-start | bytes 3735560 | tf_op jit(solution)/shard_map/ppermute | solution.py:137
  31.4 18.2 %collective-permute-start = (bf16[16,304,128]{2,1,0:T(8,128)(2,1)S(1)}, bf16[16,304,128]{2,1,0:T(8,128)(2,1)S(1)}, u32[]{:S(2)}, u32[]{:S(2)}) collective-permute-start(bf16[16,304,128]{2,1,0:T(8,128)(2,1)S(1)} %all-to-all-done.own_panel), channel_id=1, source_target_pairs={{16,32},{48,64},{80,96},{112,128},{144,160},{176,192},{208,224},{2... | collective-permute-start | bytes 3735560 | tf_op jit(solution)/shard_map/ppermute | solution.py:132
  34.3 2.3 %copy-start = (bf16[20,289,289]{2,1,0:T(8,128)(2,1)S(1)}, bf16[20,289,289]{2,1,0:T(8,128)(2,1)}, u32[]{:S(2)}) copy-start(bf16[20,289,289]{2,1,0:T(8,128)(2,1)} %operators.3) | copy-start | bytes 10022524

commit v4 on v3

--- a/solution.py
+++ b/solution.py
@@ -39,7 +39,7 @@
     return items.astype(jnp.int32), ends.astype(jnp.int32)
 
 
-def add_items(items, first, last, operators, panel, total):
+def add_items(items, first, last, operators, panel, total, ready=lambda i, seen: seen):
     coeffs = operators.shape[1]
 
     def one(i):
@@ -52,16 +52,20 @@
         total[left, :coeffs] += made[:, :128]
         total[right, :coeffs] += made[:, 128:]
 
+    seen = jnp.int32(0)
     for size in GROUPS:
 
-        def step(k, carry, first=first, size=size):
-            for part in [one(first + k * size + u) for u in range(size)]:
+        def step(k, seen, first=first, size=size):
+            base = first + k * size
+            seen = ready(base + size - 1, seen)
+            for part in [one(base + u) for u in range(size)]:
                 put(*part)
-            return carry
+            return seen
 
         full = lax.div(last - first, size)
-        lax.fori_loop(0, full, step, 0)
+        seen = lax.fori_loop(0, full, step, seen)
         first = first + full * size
+    return seen
 
 
 def spread_kernel(block, out):
@@ -73,9 +77,24 @@
         out[t, whole:] = last
 
 
-def near_kernel(items, ends, operators, own_panel, other_panel, total):
+def near_kernel(items, ends, held, own_panel, other_panel, total, operators, arrived):
+    def copy(c):
+        return pltpu.make_async_copy(held.at[c], operators.at[c], arrived.at[c])
+
+    def wait(c, carry):
+        copy(c).wait()
+        return carry
+
+    def ready(i, seen):
+        need = (items[2 * i] & 31) + 1
+        lax.fori_loop(seen, need, wait, 0)
+        return jnp.maximum(seen, need)
+
+    for c in range(held.shape[0]):
+        copy(c).start()
     total[...] = jnp.zeros_like(total)
-    add_items(items, 0, ends[0], operators, own_panel, total)
+    seen = add_items(items, 0, ends[0], operators, own_panel, total, ready)
+    lax.fori_loop(seen, held.shape[0], wait, 0)
     add_items(items, ends[0], ends[1], operators, other_panel, total)
 
 
@@ -117,34 +136,36 @@
     grp_n = lax.axis_size("grp")
     coeffs, width = multipoles.shape
     held = operators.shape[0]
-    rows = (coeffs + 16) // 16 * 16
+    rows = (coeffs + 8) // 8 * 8
     spread = pl.pallas_call(
         spread_kernel,
         out_shape=jax.ShapeDtypeStruct((own_n, rows, width), multipoles.dtype),
         in_specs=[VMEM],
         out_specs=VMEM,
         compiler_params=pltpu.CompilerParams(vmem_limit_bytes=8 * 2**20),
-    )(multipoles)
+    )(pltpu.with_memory_space_constraint(multipoles, pltpu.HBM))
     own_panel = lax.all_to_all(
         spread, "own", split_axis=0, concat_axis=0, tiled=True
     )
     across = [(i, i + 1) for i in range(1, grp_n - 1, 2)]
     far_panel = lax.ppermute(own_panel, "grp", across + [(j, i) for i, j in across])
-    target, sources, classes, owner, unused = lax.optimization_barrier(
+    target, sources, classes, owner, gathered = lax.optimization_barrier(
         (targets[:, 0], sources, classes, owners[0], own_panel)
     )
     items, ends = plan(target, sources, classes, owner, held)
-    other_panel = lax.ppermute(own_panel, "grp", [(i, i ^ 1) for i in range(grp_n)])
+    other_panel = lax.ppermute(gathered, "grp", [(i, i ^ 1) for i in range(grp_n)])
     vmem = pltpu.CompilerParams(vmem_limit_bytes=32 * 2**20)
     pair = 2 * coeffs * coeffs * width
+    kept = pltpu.with_memory_space_constraint(operators, pltpu.HBM)
     begun = pl.pallas_call(
         near_kernel,
         out_shape=jax.ShapeDtypeStruct((own_n + 1, rows, width), jnp.float32),
-        in_specs=[SMEM, SMEM, VMEM, VMEM, VMEM],
+        in_specs=[SMEM, SMEM, pl.BlockSpec(memory_space=pltpu.HBM), VMEM, VMEM],
         out_specs=VMEM,
+        scratch_shapes=[pltpu.VMEM(operators.shape, operators.dtype), pltpu.SemaphoreType.DMA((held,))],
         compiler_params=vmem,
         cost_estimate=pl.CostEstimate(flops=pair, bytes_accessed=2**16, transcendentals=0),
-    )(items, ends, operators, own_panel, other_panel)
+    )(items, ends, kept, gathered, other_panel)
     partial = pl.pallas_call(
         far_kernel,
         out_shape=jax.ShapeDtypeStruct((own_n, rows, width), jnp.int16),

time: 81.5 us -> 79.3 us (0.973)
  the two profiles are of different devices: /device:TPU:96 before, /device:TPU:225 now
where the time goes in v4:
time: 79.3 us; the launch traced here: 79 us
  blocking collectives  21.7 us (27%)
  Pallas kernels  20.2 us (25%)
  waiting for transfers between devices  19.9 us (25%)
  starting transfers between devices  16.3 us (21%)
  other arithmetic  0.85 us (1%)
    all_to_all x1, blocking collectives, per_device(): lax.all_to_all(partial, 'own', split_axis=0, concat_axis=0, tiled=True)  21.7 us
    all_to_all x1, waiting for transfers between devices, per_device(): lax.all_to_all(spread, 'own', split_axis=0, concat_axis=0, tiled=True)  17.7 us
    pallas_call x1, Pallas kernels, per_device(): pl.pallas_call(near_kernel, out_shape=jax.ShapeDtypeStruct((own_n + 1, ro...  11.5 us
    all_to_all x1, starting transfers between devices, per_device(): lax.all_to_all(spread, 'own', split_axis=0, concat_axis=0, tiled=True)  6.9 us
    pallas_call x1, Pallas kernels, per_device(): pl.pallas_call(far_kernel, out_shape=jax.ShapeDtypeStruct((own_n, rows, w...  5.67 us
    ppermute x1, starting transfers between devices, per_device(): lax.ppermute(gathered, 'grp', [(i, i ^ 1) for i in range(grp_n)])  4.73 us
    ppermute x1, starting transfers between devices, per_device(): lax.ppermute(own_panel, 'grp', across + [(j, i) for i, j in across])  4.65 us
    ppermute x1, waiting for transfers between devices, per_device(): lax.ppermute(own_panel, 'grp', across + [(j, i) for i, j in across])  2.15 us
  transfers between devices with their start and end apart: 3, of which 2 were waited for; matrix products, arithmetic and copies ran while one was open for 1% of the time, Pallas kernels for 15%

profile of v4, /device:TPU:225, one launch (start us, length us, event | category | flops | bytes accessed | tf_op | source)
XLA Modules:
  0.0 79.0 jit_solution(5019502121656387757)
XLA Ops:
  0.0 2.1 %shard_map.64 = bf16[16,296,128]{2,1,0:T(8,128)(2,1)} custom-call(bf16[289,128]{1,0:T(8,128)(2,1)} %block.1), custom_call_target="tpu_custom_call" | custom-call | tf_op jit(solution)/shard_map/pallas_call | solution.py:140
  2.1 6.9 %all-to-all-start = ((bf16[16,296,128]{2,1,0:T(8,128)(2,1)}), bf16[16,296,128]{2,1,0:T(8,128)(2,1)S(1)}, u32[]{:S(2)}, u32[]{:S(2)}) async-start(bf16[16,296,128]{2,1,0:T(8,128)(2,1)} %shard_map.64), calls=%async_computation | async-start | bytes 2424832 | tf_op jit(solution)/shard_map/all_to_all | solution.py:147
  9.0 17.7 %all-to-all-done.own_panel = bf16[16,296,128]{2,1,0:T(8,128)(2,1)S(1)} async-done(((bf16[16,296,128]{2,1,0:T(8,128)(2,1)}), bf16[16,296,128]{2,1,0:T(8,128)(2,1)S(1)}, u32[]{:S(2)}, u32[]{:S(2)}) %all-to-all-start) | async-done | bytes 1212448 | tf_op jit(solution)/shard_map/all_to_all | solution.py:147
  26.7 4.7 %collective-permute-start.1 = (bf16[16,296,128]{2,1,0:T(8,128)(2,1)S(1)}, bf16[16,296,128]{2,1,0:T(8,128)(2,1)S(1)}, u32[]{:S(2)}, u32[]{:S(2)}) collective-permute-start(bf16[16,296,128]{2,1,0:T(8,128)(2,1)S(1)} %all-to-all-done.own_panel), channel_id=1, source_target_pairs={{0,16},{16,0},{32,48},{48,32},{64,80},{80,64},{96,112},{112,96},{1... | collective-permute-start | bytes 3637256 | tf_op jit(solution)/shard_map/ppermute | solution.py:156
  31.4 0.0 copy-done
  31.5 0.0 copy-done.3
  31.5 0.1 select_reduce_fusion.2
  31.6 0.0 copy-done.1
  31.6 0.0 copy-done.2
  31.6 4.7 %collective-permute-start = (bf16[16,296,128]{2,1,0:T(8,128)(2,1)S(1)}, bf16[16,296,128]{2,1,0:T(8,128)(2,1)S(1)}, u32[]{:S(2)}, u32[]{:S(2)}) collective-permute-start(bf16[16,296,128]{2,1,0:T(8,128)(2,1)S(1)} %all-to-all-done.own_panel), channel_id=1, source_target_pairs={{16,32},{48,64},{80,96},{112,128},{144,160},{176,192},{208,224},{2... | collective-permute-start | bytes 3637256 | tf_op jit(solution)/shard_map/ppermute | solution.py:151
  36.3 0.1 convert_reduce_fusion.1
  36.4 0.1 select_reduce_fusion.1
  36.5 0.2 convert_reduce_fusion
  36.7 0.2 select_reduce_fusion.3
  36.9 0.1 select_reduce_fusion
  37.0 0.0 slice-start
  37.0 0.0 slice-start.1
  37.1 0.0 collective-permute-done.1.other_panel
  37.1 11.5 %shard_map.65.begun = f32[17,296,128]{2,1,0:T(8,128)S(1)} custom-call(s32[256]{0:T(256)S(1)} %broadcast_add_fusion.items, s32[3]{0:T(128)S(1)} %and_select_fusion.ends, bf16[20,289,289]{2,1,0:T(8,128)(2,1)} %operators.1, bf16[16,296,128]{2,1,0:T(8,128)(2,1)S(1)} %all-to-all-done.own_panel, bf16[16,296,128]{2,1,0:T(8,128)(2,1)S(1)} %collective-permute-done.1.other_panel), custom_call_target="tpu_custom_call" | custom-call | flops 21381376 | bytes 65536 | tf_op jit(solution)/shard_map/pallas_call | solution.py:160
  48.5 2.1 %collective-permute-done.panel = bf16[16,296,128]{2,1,0:T(8,128)(2,1)S(1)} collective-permute-done((bf16[16,296,128]{2,1,0:T(8,128)(2,1)S(1)}, bf16[16,296,128]{2,1,0:T(8,128)(2,1)S(1)}, u32[]{:S(2)}, u32[]{:S(2)}) %collective-permute-start) | collective-permute-done | bytes 1212448 | tf_op jit(solution)/shard_map/ppermute | solution.py:151
  50.7 0.0 slice-done
  50.7 5.7 %shard_map.66 = s16[16,296,128]{2,1,0:T(8,128)(2,1)S(1)} custom-call(s32[256]{0:T(256)S(1)} %broadcast_add_fusion.items, s32[3]{0:T(128)S(1)} %and_select_fusion.ends, bf16[20,289,289]{2,1,0:T(8,128)(2,1)S(1)} %bitcast.3, bf16[16,296,128]{2,1,0:T(8,128)(2,1)S(1)} %collective-permute-done.panel, f32[17,296,128]{2,1,0:T(8,128)S(1)} %shard_map.65.begun), custom_call_target="tpu_custom_call" | custom-call | flops 4105224192 | bytes 8388608 | tf_op jit(solution)/shard_map/pallas_call | solution.py:169
  56.4 21.7 %all_to_all.10.moved = s16[16,296,128]{2,1,0:T(8,128)(2,1)S(1)} all-to-all(s16[16,296,128]{2,1,0:T(8,128)(2,1)S(1)} %shard_map.66), channel_id=1, replica_groups=mesh['grp'=32,'own'=16] {'own'}, dimensions={0} | all-to-all | bytes 2424832 | tf_op jit(solution)/shard_map/all_to_all | solution.py:178
  78.0 1.0 %shard_map.67 = f32[289,128]{1,0:T(8,128)} custom-call(s16[16,296,128]{2,1,0:T(8,128)(2,1)S(1)} %all_to_all.10.moved), custom_call_target="tpu_custom_call" | custom-call | tf_op jit(solution)/shard_map/pallas_call | solution.py:179
  (12 shorter events, 0.1 us)
Async XLA Ops:
  2.1 29.4 %copy-start = (s32[192,1]{0,1:T(1,128)S(1)}, s32[192,1]{0,1:T(1,128)}, u32[]{:S(2)}) copy-start(s32[192,1]{0,1:T(1,128)} %param.8) | copy-start | bytes 2308
  2.1 29.4 %copy-start.3 = (s32[1,16]{1,0:T(1,128)S(1)}, s32[1,16]{1,0:T(1,128)}, u32[]{:S(2)}) copy-start(s32[1,16]{1,0:T(1,128)} %param.11) | copy-start | bytes 196
  2.1 29.5 %copy-start.1 = (s32[192]{0:T(256)S(1)}, s32[192]{0:T(256)}, u32[]{:S(2)}) copy-start(s32[192]{0:T(256)} %param.10) | copy-start | bytes 2308
  2.1 29.5 %copy-start.2 = (s32[192]{0:T(256)S(1)}, s32[192]{0:T(256)}, u32[]{:S(2)}) copy-start(s32[192]{0:T(256)} %param.9) | copy-start | bytes 2308
  2.1 24.6 %all-to-all-start = ((bf16[16,296,128]{2,1,0:T(8,128)(2,1)}), bf16[16,296,128]{2,1,0:T(8,128)(2,1)S(1)}, u32[]{:S(2)}, u32[]{:S(2)}) async-start(bf16[16,296,128]{2,1,0:T(8,128)(2,1)} %shard_map.64), calls=%async_computation | async-start | bytes 2424832 | tf_op jit(solution)/shard_map/all_to_all | solution.py:147
  26.7 10.3 %collective-permute-start.1 = (bf16[16,296,128]{2,1,0:T(8,128)(2,1)S(1)}, bf16[16,296,128]{2,1,0:T(8,128)(2,1)S(1)}, u32[]{:S(2)}, u32[]{:S(2)}) collective-permute-start(bf16[16,296,128]{2,1,0:T(8,128)(2,1)S(1)} %all-to-all-done.own_panel), channel_id=1, source_target_pairs={{0,16},{16,0},{32,48},{48,32},{64,80},{80,64},{96,112},{112,96},{1... | collective-permute-start | bytes 3637256 | tf_op jit(solution)/shard_map/ppermute | solution.py:156
  31.6 19.1 %collective-permute-start = (bf16[16,296,128]{2,1,0:T(8,128)(2,1)S(1)}, bf16[16,296,128]{2,1,0:T(8,128)(2,1)S(1)}, u32[]{:S(2)}, u32[]{:S(2)}) collective-permute-start(bf16[16,296,128]{2,1,0:T(8,128)(2,1)S(1)} %all-to-all-done.own_panel), channel_id=1, source_target_pairs={{16,32},{48,64},{80,96},{112,128},{144,160},{176,192},{208,224},{2... | collective-permute-start | bytes 3637256 | tf_op jit(solution)/shard_map/ppermute | solution.py:151
  37.0 13.7 %slice-start = ((s8[4546560]{0:T(1024)(128)(4,1)}), s8[4194304]{0:T(1024)(128)(4,1)S(1)}, s32[]{:S(2)}) async-start(s8[4546560]{0:T(1024)(128)(4,1)} %bitcast.2), calls=%async_computation.2 | async-start | bytes 8388608
  37.0 13.6 %slice-start.1 = ((s8[4546560]{0:T(1024)(128)(4,1)}), s8[352256]{0:T(1024)(128)(4,1)S(1)}, s32[]{:S(2)}) async-start(s8[4546560]{0:T(1024)(128)(4,1)} %bitcast.2), calls=%async_computation.3 | async-start | bytes 704512

commit v5 on v3

--- a/solution.py
+++ b/solution.py
@@ -2,6 +2,7 @@
 
 import jax
 import jax.numpy as jnp
+import numpy as np
 from jax import lax
 from jax.experimental import pallas as pl
 from jax.experimental.pallas import tpu as pltpu
@@ -19,13 +20,11 @@
 def plan(target, sources, classes, owners, held):
     count = target.shape[0]
     own_n = owners.shape[0]
-    odd = lax.rem(lax.axis_index("grp"), 2)
     shift = sources % 3
-    kind = jnp.where(shift == 1, 0, jnp.where((shift == 0) == (odd == 0), 2, 1))
-    local = classes - lax.axis_index("own") * held
+    local = classes % held
     dest = jnp.sum(jnp.where(target[:, None] == jnp.arange(own_n)[None, :], owners[None, :], 0), axis=1)
     packed = local + 32 * (sources // 3) + 2048 * dest
-    run = kind * held + local
+    run = shift * held + local
     pos = jnp.arange(count)
     rank = jnp.sum((run[:, None] == run[None, :]) & (pos[None, :] < pos[:, None]), axis=1, dtype=jnp.int32)
     runs = jnp.arange(3 * held)
@@ -35,7 +34,7 @@
     slot = offset + rank
     empty = 2048 * own_n
     items = empty + jnp.sum(jnp.where(slot[None, :] == jnp.arange(SLOTS)[:, None], packed[None, :] - empty, 0), axis=1)
-    ends = jnp.sum(jnp.where(runs[None, :] < held * jnp.arange(1, 4)[:, None], length[None, :], 0), axis=1) // 2
+    ends = jnp.sum(jnp.where(runs[None, :] < np.array([[held], [2 * held], [3 * held]], np.int32), length[None, :], 0), axis=1) // 2
     return items.astype(jnp.int32), ends.astype(jnp.int32)
 
 
@@ -73,17 +72,27 @@
         out[t, whole:] = last
 
 
+def ranges(ends):
+    odd = lax.rem(lax.axis_index("grp"), 2) == 1
+    low, high = (jnp.int32(0), ends[0]), (ends[1], ends[2])
+    other = [jnp.where(odd, x, y) for x, y in zip(low, high)]
+    far = [jnp.where(odd, y, x) for x, y in zip(low, high)]
+    return (ends[0], ends[1]), other, far
+
+
 def near_kernel(items, ends, operators, own_panel, other_panel, total):
+    own, other, far = ranges(ends)
     total[...] = jnp.zeros_like(total)
-    add_items(items, 0, ends[0], operators, own_panel, total)
-    add_items(items, ends[0], ends[1], operators, other_panel, total)
+    add_items(items, *own, operators, own_panel, total)
+    add_items(items, *other, operators, other_panel, total)
 
 
 def far_kernel(items, ends, operators, panel, begun, out, total):
     coeffs = operators.shape[1]
     whole = coeffs // 16 * 16
     total[...] = begun[...]
-    add_items(items, ends[1], ends[2], operators, panel, total)
+    own, other, far = ranges(ends)
+    add_items(items, *far, operators, panel, total)
 
     def code(t):
         values = total[t]
@@ -117,24 +126,24 @@
     grp_n = lax.axis_size("grp")
     coeffs, width = multipoles.shape
     held = operators.shape[0]
-    rows = (coeffs + 16) // 16 * 16
+    rows = (coeffs + 8) // 8 * 8
     spread = pl.pallas_call(
         spread_kernel,
         out_shape=jax.ShapeDtypeStruct((own_n, rows, width), multipoles.dtype),
         in_specs=[VMEM],
         out_specs=VMEM,
         compiler_params=pltpu.CompilerParams(vmem_limit_bytes=8 * 2**20),
-    )(multipoles)
+    )(pltpu.with_memory_space_constraint(multipoles, pltpu.HBM))
     own_panel = lax.all_to_all(
         spread, "own", split_axis=0, concat_axis=0, tiled=True
     )
     across = [(i, i + 1) for i in range(1, grp_n - 1, 2)]
     far_panel = lax.ppermute(own_panel, "grp", across + [(j, i) for i, j in across])
-    target, sources, classes, owner, unused = lax.optimization_barrier(
+    target, sources, classes, owner, gathered = lax.optimization_barrier(
         (targets[:, 0], sources, classes, owners[0], own_panel)
     )
     items, ends = plan(target, sources, classes, owner, held)
-    other_panel = lax.ppermute(own_panel, "grp", [(i, i ^ 1) for i in range(grp_n)])
+    other_panel = lax.ppermute(gathered, "grp", [(i, i ^ 1) for i in range(grp_n)])
     vmem = pltpu.CompilerParams(vmem_limit_bytes=32 * 2**20)
     pair = 2 * coeffs * coeffs * width
     begun = pl.pallas_call(
@@ -144,7 +153,7 @@
         out_specs=VMEM,
         compiler_params=vmem,
         cost_estimate=pl.CostEstimate(flops=pair, bytes_accessed=2**16, transcendentals=0),
-    )(items, ends, operators, own_panel, other_panel)
+    )(items, ends, operators, gathered, other_panel)
     partial = pl.pallas_call(
         far_kernel,
         out_shape=jax.ShapeDtypeStruct((own_n, rows, width), jnp.int16),

time: 81.5 us -> 77.7 us (0.953)
  the two profiles are of different devices: /device:TPU:96 before, /device:TPU:225 now
where the time goes in v5:
time: 77.7 us; the launch traced here: 77.4 us
  blocking collectives  47.5 us (61%)
  Pallas kernels  16.9 us (22%)
  starting transfers between devices  8.58 us (11%)
  local copies, waits for them, and re-layouts  2.32 us (3%)
  waiting for transfers between devices  1.06 us (1%)
  other arithmetic  0.84 us (1%)
    all_to_all x1, blocking collectives, per_device(): lax.all_to_all(spread, 'own', split_axis=0, concat_axis=0, tiled=True)  24.5 us
    all_to_all x1, blocking collectives, per_device(): lax.all_to_all(partial, 'own', split_axis=0, concat_axis=0, tiled=True)  23 us
    pallas_call x1, Pallas kernels, per_device(): pl.pallas_call(near_kernel, out_shape=jax.ShapeDtypeStruct((own_n + 1, ro...  10.3 us
    ppermute x1, starting transfers between devices, per_device(): lax.ppermute(own_panel, 'grp', across + [(j, i) for i, j in across])  4.65 us
    pallas_call x1, Pallas kernels, per_device(): pl.pallas_call(far_kernel, out_shape=jax.ShapeDtypeStruct((own_n, rows, w...  4.64 us
    ppermute x1, starting transfers between devices, per_device(): lax.ppermute(gathered, 'grp', [(i, i ^ 1) for i in range(grp_n)])  3.93 us
    unnamed x12, local copies, waits for them, and re-layouts  2.32 us
  transfers between devices with their start and end apart: 2, of which 1 were waited for; matrix products, arithmetic and copies ran while one was open for 1% of the time, Pallas kernels for 13%

profile of v5, /device:TPU:225, one launch (start us, length us, event | category | flops | bytes accessed | tf_op | source)
XLA Modules:
  0.0 77.4 jit_solution(7077470537261106474)
XLA Ops:
  0.0 1.0 %shard_map.73 = bf16[16,296,128]{2,1,0:T(8,128)(2,1)S(1)} custom-call(bf16[289,128]{1,0:T(8,128)(2,1)} %block.1), custom_call_target="tpu_custom_call" | custom-call | tf_op jit(solution)/shard_map/pallas_call | solution.py:130
  1.0 0.0 copy-start.3
  1.1 0.0 copy-start.4
  1.1 0.0 copy-start.1
  1.1 0.0 copy-start.2
  1.1 0.0 copy-start.5
  1.1 24.5 %all_to_all.10.own_panel = bf16[16,296,128]{2,1,0:T(8,128)(2,1)S(1)} all-to-all(bf16[16,296,128]{2,1,0:T(8,128)(2,1)S(1)} %shard_map.73), channel_id=1, replica_groups=mesh['grp'=32,'own'=16] {'own'}, dimensions={0} | all-to-all | bytes 2424832 | tf_op jit(solution)/shard_map/all_to_all | solution.py:137
  25.6 3.9 %collective-permute-start.1 = (bf16[16,296,128]{2,1,0:T(8,128)(2,1)S(1)}, bf16[16,296,128]{2,1,0:T(8,128)(2,1)S(1)}, u32[]{:S(2)}, u32[]{:S(2)}) collective-permute-start(bf16[16,296,128]{2,1,0:T(8,128)(2,1)S(1)} %all_to_all.10.own_panel), channel_id=1, source_target_pairs={{0,16},{16,0},{32,48},{48,32},{64,80},{80,64},{96,112},{112,96},{1... | collective-permute-start | bytes 3637256 | tf_op jit(solution)/shard_map/ppermute | solution.py:146
  29.6 0.0 copy-done.3
  29.6 0.1 select_reduce_fusion.2
  29.7 4.7 %collective-permute-start = (bf16[16,296,128]{2,1,0:T(8,128)(2,1)S(1)}, bf16[16,296,128]{2,1,0:T(8,128)(2,1)S(1)}, u32[]{:S(2)}, u32[]{:S(2)}) collective-permute-start(bf16[16,296,128]{2,1,0:T(8,128)(2,1)S(1)} %all_to_all.10.own_panel), channel_id=1, source_target_pairs={{16,32},{48,64},{80,96},{112,128},{144,160},{176,192},{208,224},{2... | collective-permute-start | bytes 3637256 | tf_op jit(solution)/shard_map/ppermute | solution.py:141
  34.4 0.1 convert_reduce_fusion.1
  34.5 0.1 select_reduce_fusion.1
  34.6 0.2 convert_reduce_fusion
  34.8 0.2 select_reduce_fusion.3
  35.0 0.1 select_reduce_fusion
  35.1 0.0 collective-permute-done.1.other_panel
  35.2 0.0 copy-start
  35.2 2.3 %copy-done = bf16[20,289,289]{2,1,0:T(8,128)(2,1)S(1)} copy-done((bf16[20,289,289]{2,1,0:T(8,128)(2,1)S(1)}, bf16[20,289,289]{2,1,0:T(8,128)(2,1)}, u32[]{:S(2)}) %copy-start) | copy-done | bytes 3340864
  37.4 10.3 %shard_map.74.begun = f32[17,296,128]{2,1,0:T(8,128)S(1)} custom-call(s32[256]{0:T(256)S(1)} %broadcast_add_fusion.items, s32[3]{0:T(128)S(1)} %and_select_fusion.ends, bf16[20,289,289]{2,1,0:T(8,128)(2,1)S(1)} %copy-done, bf16[16,296,128]{2,1,0:T(8,128)(2,1)S(1)} %all_to_all.10.own_panel, bf16[16,296,128]{2,1,0:T(8,128)(2,1)S(1)} %collective-permute-done.1.other_panel), custom_call_target="tpu_custom_call" | custom-call | flops 21381376 | bytes 65536 | tf_op jit(solution)/shard_map/pallas_call | solution.py:149
  47.7 1.1 %collective-permute-done.panel = bf16[16,296,128]{2,1,0:T(8,128)(2,1)S(1)} collective-permute-done((bf16[16,296,128]{2,1,0:T(8,128)(2,1)S(1)}, bf16[16,296,128]{2,1,0:T(8,128)(2,1)S(1)}, u32[]{:S(2)}, u32[]{:S(2)}) %collective-permute-start) | collective-permute-done | bytes 1212448 | tf_op jit(solution)/shard_map/ppermute | solution.py:141
  48.8 4.6 %shard_map.75 = s16[16,296,128]{2,1,0:T(8,128)(2,1)S(1)} custom-call(s32[256]{0:T(256)S(1)} %broadcast_add_fusion.items, s32[3]{0:T(128)S(1)} %and_select_fusion.ends, bf16[20,289,289]{2,1,0:T(8,128)(2,1)S(1)} %copy-done, bf16[16,296,128]{2,1,0:T(8,128)(2,1)S(1)} %collective-permute-done.panel, f32[17,296,128]{2,1,0:T(8,128)S(1)} %shard_map.74.begun), custom_call_target="tpu_custom_call" | custom-call | flops 4105224192 | bytes 8388608 | tf_op jit(solution)/shard_map/pallas_call | solution.py:157
  53.4 23.0 %all_to_all.11.moved = s16[16,296,128]{2,1,0:T(8,128)(2,1)S(1)} all-to-all(s16[16,296,128]{2,1,0:T(8,128)(2,1)S(1)} %shard_map.75), channel_id=1, replica_groups=mesh['grp'=32,'own'=16] {'own'}, dimensions={0} | all-to-all | bytes 2424832 | tf_op jit(solution)/shard_map/all_to_all | solution.py:166
  76.4 1.0 %shard_map.76 = f32[289,128]{1,0:T(8,128)} custom-call(s16[16,296,128]{2,1,0:T(8,128)(2,1)S(1)} %all_to_all.11.moved), custom_call_target="tpu_custom_call" | custom-call | tf_op jit(solution)/shard_map/pallas_call | solution.py:167
  (9 shorter events, 0.1 us)
Async XLA Ops:
  1.0 28.5 %copy-start.3 = (s32[192,1]{0,1:T(1,128)S(1)}, s32[192,1]{0,1:T(1,128)}, u32[]{:S(2)}) copy-start(s32[192,1]{0,1:T(1,128)} %param.9) | copy-start | bytes 2308
  1.1 28.5 %copy-start.4 = (s32[1,16]{1,0:T(1,128)S(1)}, s32[1,16]{1,0:T(1,128)}, u32[]{:S(2)}) copy-start(s32[1,16]{1,0:T(1,128)} %param.12) | copy-start | bytes 196
  1.1 28.6 %copy-start.1 = (s32[192]{0:T(256)S(1)}, s32[192]{0:T(256)}, u32[]{:S(2)}) copy-start(s32[192]{0:T(256)} %param.10) | copy-start | bytes 2308
  1.1 28.6 %copy-start.2 = (s32[192]{0:T(256)S(1)}, s32[192]{0:T(256)}, u32[]{:S(2)}) copy-start(s32[192]{0:T(256)} %param.11) | copy-start | bytes 2308
  1.1 33.7 %copy-start.5 = (s32[3]{0:T(128)S(1)}, s32[3]{0:T(128)}, u32[]{:S(2)}) copy-start(s32[3]{0:T(128)} %constant.71) | copy-start | bytes 40
  25.6 9.5 %collective-permute-start.1 = (bf16[16,296,128]{2,1,0:T(8,128)(2,1)S(1)}, bf16[16,296,128]{2,1,0:T(8,128)(2,1)S(1)}, u32[]{:S(2)}, u32[]{:S(2)}) collective-permute-start(bf16[16,296,128]{2,1,0:T(8,128)(2,1)S(1)} %all_to_all.10.own_panel), channel_id=1, source_target_pairs={{0,16},{16,0},{32,48},{48,32},{64,80},{80,64},{96,112},{112,96},{1... | collective-permute-start | bytes 3637256 | tf_op jit(solution)/shard_map/ppermute | solution.py:146
  29.7 19.1 %collective-permute-start = (bf16[16,296,128]{2,1,0:T(8,128)(2,1)S(1)}, bf16[16,296,128]{2,1,0:T(8,128)(2,1)S(1)}, u32[]{:S(2)}, u32[]{:S(2)}) collective-permute-start(bf16[16,296,128]{2,1,0:T(8,128)(2,1)S(1)} %all_to_all.10.own_panel), channel_id=1, source_target_pairs={{16,32},{48,64},{80,96},{112,128},{144,160},{176,192},{208,224},{2... | collective-permute-start | bytes 3637256 | tf_op jit(solution)/shard_map/ppermute | solution.py:141
  35.2 2.3 %copy-start = (bf16[20,289,289]{2,1,0:T(8,128)(2,1)S(1)}, bf16[20,289,289]{2,1,0:T(8,128)(2,1)}, u32[]{:S(2)}) copy-start(bf16[20,289,289]{2,1,0:T(8,128)(2,1)} %operators.3) | copy-start | bytes 10022524

commit v6 on v5

--- a/solution.py
+++ b/solution.py
@@ -8,7 +8,7 @@
 from jax.experimental.pallas import tpu as pltpu
 from jax.sharding import PartitionSpec as P
 
-GROUPS = (16, 4, 1)
+GROUPS = (16, 8, 4, 2, 1)
 SLOTS = 256
 LEVELS = 32000.0
 LEVEL_BITS = math.log2(LEVELS)
@@ -80,6 +80,11 @@
     return (ends[0], ends[1]), other, far
 
 
+def copy_kernel(panel, out):
+    for t in range(out.shape[0]):
+        out[t] = panel[t]
+
+
 def near_kernel(items, ends, operators, own_panel, other_panel, total):
     own, other, far = ranges(ends)
     total[...] = jnp.zeros_like(total)
@@ -138,12 +143,19 @@
         spread, "own", split_axis=0, concat_axis=0, tiled=True
     )
     across = [(i, i + 1) for i in range(1, grp_n - 1, 2)]
-    far_panel = lax.ppermute(own_panel, "grp", across + [(j, i) for i, j in across])
+    other_panel = lax.ppermute(own_panel, "grp", [(i, i ^ 1) for i in range(grp_n)])
     target, sources, classes, owner, gathered = lax.optimization_barrier(
         (targets[:, 0], sources, classes, owners[0], own_panel)
     )
     items, ends = plan(target, sources, classes, owner, held)
-    other_panel = lax.ppermute(gathered, "grp", [(i, i ^ 1) for i in range(grp_n)])
+    leaving = pl.pallas_call(
+        copy_kernel,
+        out_shape=jax.ShapeDtypeStruct(own_panel.shape, own_panel.dtype),
+        in_specs=[VMEM],
+        out_specs=VMEM,
+        compiler_params=pltpu.CompilerParams(vmem_limit_bytes=8 * 2**20),
+    )(gathered)
+    far_panel = lax.ppermute(leaving, "grp", across + [(j, i) for i, j in across])
     vmem = pltpu.CompilerParams(vmem_limit_bytes=32 * 2**20)
     pair = 2 * coeffs * coeffs * width
     begun = pl.pallas_call(

time: 77.7 us -> 75.9 us (0.977)
  the two profiles are of different devices: /device:TPU:225 before, /device:TPU:96 now
where the time goes in v6:
time: 75.9 us; the launch traced here: 75.7 us
  blocking collectives  49.2 us (65%)
  Pallas kernels  16.7 us (22%)
  starting transfers between devices  7.06 us (9%)
  waiting for transfers between devices  1.72 us (2%)
  other arithmetic  0.84 us (1%)
    all_to_all x1, blocking collectives, per_device(): lax.all_to_all(spread, 'own', split_axis=0, concat_axis=0, tiled=True)  26 us
    all_to_all x1, blocking collectives, per_device(): lax.all_to_all(partial, 'own', split_axis=0, concat_axis=0, tiled=True)  23.2 us
    pallas_call x1, Pallas kernels, per_device(): pl.pallas_call(near_kernel, out_shape=jax.ShapeDtypeStruct((own_n + 1, ro...  9.33 us
    pallas_call x1, Pallas kernels, per_device(): pl.pallas_call(far_kernel, out_shape=jax.ShapeDtypeStruct((own_n, rows, w...  5.28 us
    ppermute x1, starting transfers between devices, per_device(): lax.ppermute(own_panel, 'grp', [(i, i ^ 1) for i in range(grp_n)])  5.14 us
    ppermute x1, starting transfers between devices, per_device(): lax.ppermute(leaving, 'grp', across + [(j, i) for i, j in across])  1.92 us
    ppermute x1, waiting for transfers between devices, per_device(): lax.ppermute(own_panel, 'grp', [(i, i ^ 1) for i in range(grp_n)])  1.72 us
  transfers between devices with their start and end apart: 2, of which 1 were waited for; matrix products, arithmetic and copies ran while one was open for 1% of the time, Pallas kernels for 12%

profile of v6, /device:TPU:96, one launch (start us, length us, event | category | flops | bytes accessed | tf_op | source)
XLA Modules:
  0.0 75.7 jit_solution(17710880943058746413)
XLA Ops:
  0.0 1.0 %shard_map.73 = bf16[16,296,128]{2,1,0:T(8,128)(2,1)S(1)} custom-call(bf16[289,128]{1,0:T(8,128)(2,1)} %block.1), custom_call_target="tpu_custom_call" | custom-call | tf_op jit(solution)/shard_map/pallas_call | solution.py:135
  1.0 0.0 copy-start
  1.1 26.0 %all_to_all.10.panel.own_panel = bf16[16,296,128]{2,1,0:T(8,128)(2,1)S(1)} all-to-all(bf16[16,296,128]{2,1,0:T(8,128)(2,1)S(1)} %shard_map.73), channel_id=1, replica_groups=mesh['grp'=32,'own'=16] {'own'}, dimensions={0} | all-to-all | bytes 2424832 | tf_op jit(solution)/shard_map/all_to_all | solution.py:142
  27.1 0.0 copy-start.5
  27.1 0.1 shard_map.74
  27.2 1.9 %collective-permute-start = (bf16[16,296,128]{2,1,0:T(8,128)(2,1)S(1)}, bf16[16,296,128]{2,1,0:T(8,128)(2,1)S(1)}, u32[]{:S(2)}, u32[]{:S(2)}) collective-permute-start(bf16[16,296,128]{2,1,0:T(8,128)(2,1)S(1)} %shard_map.74), channel_id=1, source_target_pairs={{16,32},{48,64},{80,96},{112,128},{144,160},{176,192},{208,224},{2... | collective-permute-start | bytes 3637256 | tf_op jit(solution)/shard_map/ppermute | solution.py:158
  29.1 0.0 copy-done.3
  29.1 0.0 copy-done.4
  29.1 0.1 select_reduce_fusion.2
  29.2 0.0 copy-done.1
  29.2 0.0 copy-done.2
  29.2 5.1 %collective-permute-start.1 = (bf16[16,296,128]{2,1,0:T(8,128)(2,1)S(1)}, bf16[16,296,128]{2,1,0:T(8,128)(2,1)S(1)}, u32[]{:S(2)}, u32[]{:S(2)}) collective-permute-start(bf16[16,296,128]{2,1,0:T(8,128)(2,1)S(1)} %all_to_all.10.panel.own_panel), channel_id=1, source_target_pairs={{0,16},{16,0},{32,48},{48,32},{64,80},{80,64},{96,112},{112,96},{1... | collective-permute-start | bytes 3637256 | tf_op jit(solution)/shard_map/ppermute | solution.py:146
  34.4 0.1 convert_reduce_fusion.1
  34.5 0.1 select_reduce_fusion.1
  34.6 0.2 convert_reduce_fusion
  34.8 0.0 copy-done.5
  34.8 0.2 select_reduce_fusion.3
  35.0 0.1 select_reduce_fusion
  35.2 1.7 %collective-permute-done.1.other_panel = bf16[16,296,128]{2,1,0:T(8,128)(2,1)S(1)} collective-permute-done((bf16[16,296,128]{2,1,0:T(8,128)(2,1)S(1)}, bf16[16,296,128]{2,1,0:T(8,128)(2,1)S(1)}, u32[]{:S(2)}, u32[]{:S(2)}) %collective-permute-start.1) | collective-permute-done | bytes 1212448 | tf_op jit(solution)/shard_map/ppermute | solution.py:146
  36.9 9.3 %shard_map.75.begun = f32[17,296,128]{2,1,0:T(8,128)S(1)} custom-call(s32[256]{0:T(256)S(1)} %broadcast_add_fusion.items, s32[3]{0:T(128)S(1)} %and_select_fusion.ends, bf16[20,289,289]{2,1,0:T(8,128)(2,1)S(1)} %copy-done, bf16[16,296,128]{2,1,0:T(8,128)(2,1)S(1)} %all_to_all.10.panel.own_panel, bf16[16,296,128]{2,1,0:T(8,128)(2,1)S(1)} %collective-permute-done.1.other_panel), custom_call_target="tpu_custom_call" | custom-call | flops 21381376 | bytes 65536 | tf_op jit(solution)/shard_map/pallas_call | solution.py:161
  46.2 0.0 collective-permute-done.panel
  46.2 5.3 %shard_map.76 = s16[16,296,128]{2,1,0:T(8,128)(2,1)S(1)} custom-call(s32[256]{0:T(256)S(1)} %broadcast_add_fusion.items, s32[3]{0:T(128)S(1)} %and_select_fusion.ends, bf16[20,289,289]{2,1,0:T(8,128)(2,1)S(1)} %copy-done, bf16[16,296,128]{2,1,0:T(8,128)(2,1)S(1)} %collective-permute-done.panel, f32[17,296,128]{2,1,0:T(8,128)S(1)} %shard_map.75.begun), custom_call_target="tpu_custom_call" | custom-call | flops 4105224192 | bytes 8388608 | tf_op jit(solution)/shard_map/pallas_call | solution.py:169
  51.5 23.2 %all_to_all.11.moved = s16[16,296,128]{2,1,0:T(8,128)(2,1)S(1)} all-to-all(s16[16,296,128]{2,1,0:T(8,128)(2,1)S(1)} %shard_map.76), channel_id=1, replica_groups=mesh['grp'=32,'own'=16] {'own'}, dimensions={0} | all-to-all | bytes 2424832 | tf_op jit(solution)/shard_map/all_to_all | solution.py:178
  74.7 1.0 %shard_map.77 = f32[289,128]{1,0:T(8,128)} custom-call(s16[16,296,128]{2,1,0:T(8,128)(2,1)S(1)} %all_to_all.11.moved), custom_call_target="tpu_custom_call" | custom-call | tf_op jit(solution)/shard_map/pallas_call | solution.py:179
  (10 shorter events, 0.1 us)
Async XLA Ops:
  1.0 35.9 %copy-start = (bf16[20,289,289]{2,1,0:T(8,128)(2,1)S(1)}, bf16[20,289,289]{2,1,0:T(8,128)(2,1)}, u32[]{:S(2)}) copy-start(bf16[20,289,289]{2,1,0:T(8,128)(2,1)} %operators.3) | copy-start | bytes 10022524
  27.1 2.0 %copy-start.3 = (s32[192,1]{0,1:T(1,128)S(1)}, s32[192,1]{0,1:T(1,128)}, u32[]{:S(2)}) copy-start(s32[192,1]{0,1:T(1,128)} %param.9) | copy-start | bytes 2308
  27.1 2.0 %copy-start.4 = (s32[1,16]{1,0:T(1,128)S(1)}, s32[1,16]{1,0:T(1,128)}, u32[]{:S(2)}) copy-start(s32[1,16]{1,0:T(1,128)} %param.12) | copy-start | bytes 196
  27.1 2.1 %copy-start.1 = (s32[192]{0:T(256)S(1)}, s32[192]{0:T(256)}, u32[]{:S(2)}) copy-start(s32[192]{0:T(256)} %param.10) | copy-start | bytes 2308
  27.1 2.2 %copy-start.2 = (s32[192]{0:T(256)S(1)}, s32[192]{0:T(256)}, u32[]{:S(2)}) copy-start(s32[192]{0:T(256)} %param.11) | copy-start | bytes 2308
  27.1 7.8 %copy-start.5 = (s32[3]{0:T(128)S(1)}, s32[3]{0:T(128)}, u32[]{:S(2)}) copy-start(s32[3]{0:T(128)} %constant.71) | copy-start | bytes 40
  27.2 19.1 %collective-permute-start = (bf16[16,296,128]{2,1,0:T(8,128)(2,1)S(1)}, bf16[16,296,128]{2,1,0:T(8,128)(2,1)S(1)}, u32[]{:S(2)}, u32[]{:S(2)}) collective-permute-start(bf16[16,296,128]{2,1,0:T(8,128)(2,1)S(1)} %shard_map.74), channel_id=1, source_target_pairs={{16,32},{48,64},{80,96},{112,128},{144,160},{176,192},{208,224},{2... | collective-permute-start | bytes 3637256 | tf_op jit(solution)/shard_map/ppermute | solution.py:158
  29.2 7.6 %collective-permute-start.1 = (bf16[16,296,128]{2,1,0:T(8,128)(2,1)S(1)}, bf16[16,296,128]{2,1,0:T(8,128)(2,1)S(1)}, u32[]{:S(2)}, u32[]{:S(2)}) collective-permute-start(bf16[16,296,128]{2,1,0:T(8,128)(2,1)S(1)} %all_to_all.10.panel.own_panel), channel_id=1, source_target_pairs={{0,16},{16,0},{32,48},{48,32},{64,80},{80,64},{96,112},{112,96},{1... | collective-permute-start | bytes 3637256 | tf_op jit(solution)/shard_map/ppermute | solution.py:146

commit v7 on v6

--- a/solution.py
+++ b/solution.py
@@ -10,6 +10,7 @@
 
 GROUPS = (16, 8, 4, 2, 1)
 SLOTS = 256
+CHUNK = 96
 LEVELS = 32000.0
 LEVEL_BITS = math.log2(LEVELS)
 FINE = 64.0
@@ -100,13 +101,18 @@
     add_items(items, *far, operators, panel, total)
 
     def code(t):
-        values = total[t]
-        top = jnp.maximum(jnp.max(jnp.abs(values), axis=0, keepdims=True), 1e-32)
+        top = jnp.full((1, out.shape[2]), 1e-32, jnp.float32)
+        for low in range(0, whole, CHUNK):
+            top = jnp.maximum(top, jnp.max(jnp.abs(total[t, low : low + CHUNK]), axis=0, keepdims=True))
+        last = total[t, whole:]
+        top = jnp.maximum(top, jnp.max(jnp.abs(last), axis=0, keepdims=True))
         level = jnp.ceil(jnp.log2(top) * FINE)
-        steps = jnp.round(values * jnp.exp2(level * (-1.0 / FINE) + LEVEL_BITS))
-        row = lax.broadcasted_iota(jnp.int32, steps[whole:].shape, 0)
-        out[t, :whole] = steps[:whole].astype(jnp.int32).astype(jnp.int16)
-        out[t, whole:] = jnp.where(row < coeffs - whole, steps[whole:], level).astype(jnp.int32).astype(jnp.int16)
+        scale = jnp.exp2(level * (-1.0 / FINE) + LEVEL_BITS)
+        for low in range(0, whole, CHUNK):
+            steps = jnp.round(total[t, low : low + CHUNK] * scale)
+            out[t, low : low + CHUNK] = steps.astype(jnp.int32).astype(jnp.int16)
+        row = lax.broadcasted_iota(jnp.int32, last.shape, 0)
+        out[t, whole:] = jnp.where(row < coeffs - whole, jnp.round(last * scale), level).astype(jnp.int32).astype(jnp.int16)
 
     def some(k, carry):
         for u in range(4):
@@ -118,12 +124,25 @@
 
 def sum_kernel(moved, out):
     coeffs = out.shape[0]
-    result = jnp.zeros(out.shape, jnp.float32)
-    for j in range(moved.shape[0]):
-        values = moved[j].astype(jnp.int32).astype(jnp.float32)
-        scale = jnp.exp2(values[coeffs : coeffs + 1] * (1.0 / FINE)) * (1.0 / LEVELS)
-        result = result + values[:coeffs] * scale
-    out[...] = result
+    whole = coeffs // 16 * 16
+    many = range(moved.shape[0])
+
+    def values(j, low, high):
+        return moved[j, low:high].astype(jnp.int32).astype(jnp.float32)
+
+    lasts = [values(j, whole, moved.shape[1]) for j in many]
+    scales = [
+        jnp.exp2(last[coeffs - whole : coeffs - whole + 1] * (1.0 / FINE)) * (1.0 / LEVELS) for last in lasts
+    ]
+    for low in range(0, whole, CHUNK):
+        result = values(0, low, low + CHUNK) * scales[0]
+        for j in many[1:]:
+            result = result + values(j, low, low + CHUNK) * scales[j]
+        out[low : low + CHUNK] = result
+    result = lasts[0][: coeffs - whole] * scales[0]
+    for j in many[1:]:
+        result = result + lasts[j][: coeffs - whole] * scales[j]
+    out[whole:] = result
 
 
 def per_device(multipoles, operators, targets, sources, classes, owners):

time: 75.9 us -> 75.8 us (level)
    pallas_call x1, Pallas kernels: 9.33 us -> 10.3 us  [per_device(): pl.pallas_call(near_kernel, out_shape=jax.ShapeDtypeStruct((own_n + 1, ro...]
  transfers between devices with their start and end apart: 2 -> 2, of which waited for: 1 -> 1; matrix products, arithmetic and copies ran while one was open for 1% -> 1% of each run, Pallas kernels for 12% -> 14%
where the time goes in v7:
time: 75.8 us; the launch traced here: 75.4 us
  blocking collectives  48.6 us (64%)
  Pallas kernels  17 us (22%)
  starting transfers between devices  7.06 us (9%)
  waiting for transfers between devices  1.72 us (2%)
  other arithmetic  0.84 us (1%)
    all_to_all x1, blocking collectives, per_device(): lax.all_to_all(spread, 'own', split_axis=0, concat_axis=0, tiled=True)  26 us
    all_to_all x1, blocking collectives, per_device(): lax.all_to_all(partial, 'own', split_axis=0, concat_axis=0, tiled=True)  22.6 us
    pallas_call x1, Pallas kernels, per_device(): pl.pallas_call(near_kernel, out_shape=jax.ShapeDtypeStruct((own_n + 1, ro...  10.3 us
    ppermute x1, starting transfers between devices, per_device(): lax.ppermute(own_panel, 'grp', [(i, i ^ 1) for i in range(grp_n)])  5.14 us
    pallas_call x1, Pallas kernels, per_device(): pl.pallas_call(far_kernel, out_shape=jax.ShapeDtypeStruct((own_n, rows, w...  4.63 us
    ppermute x1, starting transfers between devices, per_device(): lax.ppermute(leaving, 'grp', across + [(j, i) for i, j in across])  1.92 us
    ppermute x1, waiting for transfers between devices, per_device(): lax.ppermute(own_panel, 'grp', [(i, i ^ 1) for i in range(grp_n)])  1.72 us
  transfers between devices with their start and end apart: 2, of which 1 were waited for; matrix products, arithmetic and copies ran while one was open for 1% of the time, Pallas kernels for 14%

profile of v7, /device:TPU:96, one launch (start us, length us, event | category | flops | bytes accessed | tf_op | source)
XLA Modules:
  0.0 75.4 jit_solution(17878047090132015790)
XLA Ops:
  0.0 1.0 %shard_map.73 = bf16[16,296,128]{2,1,0:T(8,128)(2,1)S(1)} custom-call(bf16[289,128]{1,0:T(8,128)(2,1)} %block.1), custom_call_target="tpu_custom_call" | custom-call | tf_op jit(solution)/shard_map/pallas_call | solution.py:154
  1.0 0.0 copy-start
  1.1 26.0 %all_to_all.10.panel.own_panel = bf16[16,296,128]{2,1,0:T(8,128)(2,1)S(1)} all-to-all(bf16[16,296,128]{2,1,0:T(8,128)(2,1)S(1)} %shard_map.73), channel_id=1, replica_groups=mesh['grp'=32,'own'=16] {'own'}, dimensions={0} | all-to-all | bytes 2424832 | tf_op jit(solution)/shard_map/all_to_all | solution.py:161
  27.1 0.0 copy-start.5
  27.1 0.1 shard_map.74
  27.2 1.9 %collective-permute-start = (bf16[16,296,128]{2,1,0:T(8,128)(2,1)S(1)}, bf16[16,296,128]{2,1,0:T(8,128)(2,1)S(1)}, u32[]{:S(2)}, u32[]{:S(2)}) collective-permute-start(bf16[16,296,128]{2,1,0:T(8,128)(2,1)S(1)} %shard_map.74), channel_id=1, source_target_pairs={{16,32},{48,64},{80,96},{112,128},{144,160},{176,192},{208,224},{2... | collective-permute-start | bytes 3637256 | tf_op jit(solution)/shard_map/ppermute | solution.py:177
  29.1 0.0 copy-done.3
  29.1 0.0 copy-done.4
  29.1 0.1 select_reduce_fusion.2
  29.2 0.0 copy-done.1
  29.2 0.0 copy-done.2
  29.2 5.1 %collective-permute-start.1 = (bf16[16,296,128]{2,1,0:T(8,128)(2,1)S(1)}, bf16[16,296,128]{2,1,0:T(8,128)(2,1)S(1)}, u32[]{:S(2)}, u32[]{:S(2)}) collective-permute-start(bf16[16,296,128]{2,1,0:T(8,128)(2,1)S(1)} %all_to_all.10.panel.own_panel), channel_id=1, source_target_pairs={{0,16},{16,0},{32,48},{48,32},{64,80},{80,64},{96,112},{112,96},{1... | collective-permute-start | bytes 3637256 | tf_op jit(solution)/shard_map/ppermute | solution.py:165
  34.4 0.1 convert_reduce_fusion.1
  34.5 0.1 select_reduce_fusion.1
  34.6 0.2 convert_reduce_fusion
  34.8 0.0 copy-done.5
  34.8 0.2 select_reduce_fusion.3
  35.0 0.1 select_reduce_fusion
  35.2 1.7 %collective-permute-done.1.other_panel = bf16[16,296,128]{2,1,0:T(8,128)(2,1)S(1)} collective-permute-done((bf16[16,296,128]{2,1,0:T(8,128)(2,1)S(1)}, bf16[16,296,128]{2,1,0:T(8,128)(2,1)S(1)}, u32[]{:S(2)}, u32[]{:S(2)}) %collective-permute-start.1) | collective-permute-done | bytes 1212448 | tf_op jit(solution)/shard_map/ppermute | solution.py:165
  36.9 10.3 %shard_map.75.begun = f32[17,296,128]{2,1,0:T(8,128)S(1)} custom-call(s32[256]{0:T(256)S(1)} %broadcast_add_fusion.items, s32[3]{0:T(128)S(1)} %and_select_fusion.ends, bf16[20,289,289]{2,1,0:T(8,128)(2,1)S(1)} %copy-done, bf16[16,296,128]{2,1,0:T(8,128)(2,1)S(1)} %all_to_all.10.panel.own_panel, bf16[16,296,128]{2,1,0:T(8,128)(2,1)S(1)} %collective-permute-done.1.other_panel), custom_call_target="tpu_custom_call" | custom-call | flops 21381376 | bytes 65536 | tf_op jit(solution)/shard_map/pallas_call | solution.py:180
  47.2 0.0 collective-permute-done.panel
  47.2 4.6 %shard_map.76 = s16[16,296,128]{2,1,0:T(8,128)(2,1)S(1)} custom-call(s32[256]{0:T(256)S(1)} %broadcast_add_fusion.items, s32[3]{0:T(128)S(1)} %and_select_fusion.ends, bf16[20,289,289]{2,1,0:T(8,128)(2,1)S(1)} %copy-done, bf16[16,296,128]{2,1,0:T(8,128)(2,1)S(1)} %collective-permute-done.panel, f32[17,296,128]{2,1,0:T(8,128)S(1)} %shard_map.75.begun), custom_call_target="tpu_custom_call" | custom-call | flops 4105224192 | bytes 8388608 | tf_op jit(solution)/shard_map/pallas_call | solution.py:188
  51.8 22.6 %all_to_all.11.moved = s16[16,296,128]{2,1,0:T(8,128)(2,1)S(1)} all-to-all(s16[16,296,128]{2,1,0:T(8,128)(2,1)S(1)} %shard_map.76), channel_id=1, replica_groups=mesh['grp'=32,'own'=16] {'own'}, dimensions={0} | all-to-all | bytes 2424832 | tf_op jit(solution)/shard_map/all_to_all | solution.py:197
  74.4 1.0 %shard_map.77 = f32[289,128]{1,0:T(8,128)} custom-call(s16[16,296,128]{2,1,0:T(8,128)(2,1)S(1)} %all_to_all.11.moved), custom_call_target="tpu_custom_call" | custom-call | tf_op jit(solution)/shard_map/pallas_call | solution.py:198
  (10 shorter events, 0.1 us)
Async XLA Ops:
  1.0 35.9 %copy-start = (bf16[20,289,289]{2,1,0:T(8,128)(2,1)S(1)}, bf16[20,289,289]{2,1,0:T(8,128)(2,1)}, u32[]{:S(2)}) copy-start(bf16[20,289,289]{2,1,0:T(8,128)(2,1)} %operators.3) | copy-start | bytes 10022524
  27.1 2.0 %copy-start.3 = (s32[192,1]{0,1:T(1,128)S(1)}, s32[192,1]{0,1:T(1,128)}, u32[]{:S(2)}) copy-start(s32[192,1]{0,1:T(1,128)} %param.9) | copy-start | bytes 2308
  27.1 2.0 %copy-start.4 = (s32[1,16]{1,0:T(1,128)S(1)}, s32[1,16]{1,0:T(1,128)}, u32[]{:S(2)}) copy-start(s32[1,16]{1,0:T(1,128)} %param.12) | copy-start | bytes 196
  27.1 2.1 %copy-start.1 = (s32[192]{0:T(256)S(1)}, s32[192]{0:T(256)}, u32[]{:S(2)}) copy-start(s32[192]{0:T(256)} %param.10) | copy-start | bytes 2308
  27.1 2.2 %copy-start.2 = (s32[192]{0:T(256)S(1)}, s32[192]{0:T(256)}, u32[]{:S(2)}) copy-start(s32[192]{0:T(256)} %param.11) | copy-start | bytes 2308
  27.1 7.8 %copy-start.5 = (s32[3]{0:T(128)S(1)}, s32[3]{0:T(128)}, u32[]{:S(2)}) copy-start(s32[3]{0:T(128)} %constant.71) | copy-start | bytes 40
  27.2 20.0 %collective-permute-start = (bf16[16,296,128]{2,1,0:T(8,128)(2,1)S(1)}, bf16[16,296,128]{2,1,0:T(8,128)(2,1)S(1)}, u32[]{:S(2)}, u32[]{:S(2)}) collective-permute-start(bf16[16,296,128]{2,1,0:T(8,128)(2,1)S(1)} %shard_map.74), channel_id=1, source_target_pairs={{16,32},{48,64},{80,96},{112,128},{144,160},{176,192},{208,224},{2... | collective-permute-start | bytes 3637256 | tf_op jit(solution)/shard_map/ppermute | solution.py:177
  29.2 7.6 %collective-permute-start.1 = (bf16[16,296,128]{2,1,0:T(8,128)(2,1)S(1)}, bf16[16,296,128]{2,1,0:T(8,128)(2,1)S(1)}, u32[]{:S(2)}, u32[]{:S(2)}) collective-permute-start(bf16[16,296,128]{2,1,0:T(8,128)(2,1)S(1)} %all_to_all.10.panel.own_panel), channel_id=1, source_target_pairs={{0,16},{16,0},{32,48},{48,32},{64,80},{80,64},{96,112},{112,96},{1... | collective-permute-start | bytes 3637256 | tf_op jit(solution)/shard_map/ppermute | solution.py:165

commit v8 on v7

--- a/solution.py
+++ b/solution.py
@@ -114,12 +114,8 @@
         row = lax.broadcasted_iota(jnp.int32, last.shape, 0)
         out[t, whole:] = jnp.where(row < coeffs - whole, jnp.round(last * scale), level).astype(jnp.int32).astype(jnp.int16)
 
-    def some(k, carry):
-        for u in range(4):
-            code(4 * k + u)
-        return carry
-
-    lax.fori_loop(0, out.shape[0] // 4, some, 0)
+    for t in range(out.shape[0]):
+        code(t)
 
 
 def sum_kernel(moved, out):

time: 75.8 us -> 75.7 us (level)
  transfers between devices with their start and end apart: 2 -> 2, of which waited for: 1 -> 1; matrix products, arithmetic and copies ran while one was open for 1% -> 1% of each run, Pallas kernels for 14% -> 13%
where the time goes in v8:
time: 75.7 us; the launch traced here: 75.5 us
  blocking collectives  48.5 us (64%)
  Pallas kernels  17.2 us (23%)
  starting transfers between devices  7.06 us (9%)
  waiting for transfers between devices  1.72 us (2%)
  other arithmetic  0.84 us (1%)
    all_to_all x1, blocking collectives, per_device(): lax.all_to_all(spread, 'own', split_axis=0, concat_axis=0, tiled=True)  26 us
    all_to_all x1, blocking collectives, per_device(): lax.all_to_all(partial, 'own', split_axis=0, concat_axis=0, tiled=True)  22.5 us
    pallas_call x1, Pallas kernels, per_device(): pl.pallas_call(near_kernel, out_shape=jax.ShapeDtypeStruct((own_n + 1, ro...  9.87 us
    pallas_call x1, Pallas kernels, per_device(): pl.pallas_call(far_kernel, out_shape=jax.ShapeDtypeStruct((own_n, rows, w...  5.18 us
    ppermute x1, starting transfers between devices, per_device(): lax.ppermute(own_panel, 'grp', [(i, i ^ 1) for i in range(grp_n)])  5.14 us
    ppermute x1, starting transfers between devices, per_device(): lax.ppermute(leaving, 'grp', across + [(j, i) for i, j in across])  1.92 us
    ppermute x1, waiting for transfers between devices, per_device(): lax.ppermute(own_panel, 'grp', [(i, i ^ 1) for i in range(grp_n)])  1.72 us
  transfers between devices with their start and end apart: 2, of which 1 were waited for; matrix products, arithmetic and copies ran while one was open for 1% of the time, Pallas kernels for 13%

profile of v8, /device:TPU:96, one launch (start us, length us, event | category | flops | bytes accessed | tf_op | source)
XLA Modules:
  0.0 75.5 jit_solution(9295595035443134584)
XLA Ops:
  0.0 1.0 %shard_map.73 = bf16[16,296,128]{2,1,0:T(8,128)(2,1)S(1)} custom-call(bf16[289,128]{1,0:T(8,128)(2,1)} %block.1), custom_call_target="tpu_custom_call" | custom-call | tf_op jit(solution)/shard_map/pallas_call | solution.py:150
  1.0 0.0 copy-start
  1.1 26.0 %all_to_all.10.panel.own_panel = bf16[16,296,128]{2,1,0:T(8,128)(2,1)S(1)} all-to-all(bf16[16,296,128]{2,1,0:T(8,128)(2,1)S(1)} %shard_map.73), channel_id=1, replica_groups=mesh['grp'=32,'own'=16] {'own'}, dimensions={0} | all-to-all | bytes 2424832 | tf_op jit(solution)/shard_map/all_to_all | solution.py:157
  27.1 0.0 copy-start.5
  27.1 0.1 shard_map.74
  27.2 1.9 %collective-permute-start = (bf16[16,296,128]{2,1,0:T(8,128)(2,1)S(1)}, bf16[16,296,128]{2,1,0:T(8,128)(2,1)S(1)}, u32[]{:S(2)}, u32[]{:S(2)}) collective-permute-start(bf16[16,296,128]{2,1,0:T(8,128)(2,1)S(1)} %shard_map.74), channel_id=1, source_target_pairs={{16,32},{48,64},{80,96},{112,128},{144,160},{176,192},{208,224},{2... | collective-permute-start | bytes 3637256 | tf_op jit(solution)/shard_map/ppermute | solution.py:173
  29.1 0.0 copy-done.3
  29.1 0.0 copy-done.4
  29.1 0.1 select_reduce_fusion.2
  29.2 0.0 copy-done.1
  29.2 0.0 copy-done.2
  29.2 5.1 %collective-permute-start.1 = (bf16[16,296,128]{2,1,0:T(8,128)(2,1)S(1)}, bf16[16,296,128]{2,1,0:T(8,128)(2,1)S(1)}, u32[]{:S(2)}, u32[]{:S(2)}) collective-permute-start(bf16[16,296,128]{2,1,0:T(8,128)(2,1)S(1)} %all_to_all.10.panel.own_panel), channel_id=1, source_target_pairs={{0,16},{16,0},{32,48},{48,32},{64,80},{80,64},{96,112},{112,96},{1... | collective-permute-start | bytes 3637256 | tf_op jit(solution)/shard_map/ppermute | solution.py:161
  34.4 0.1 convert_reduce_fusion.1
  34.5 0.1 select_reduce_fusion.1
  34.6 0.2 convert_reduce_fusion
  34.8 0.2 select_reduce_fusion.3
  35.0 0.1 select_reduce_fusion
  35.2 1.7 %collective-permute-done.1.other_panel = bf16[16,296,128]{2,1,0:T(8,128)(2,1)S(1)} collective-permute-done((bf16[16,296,128]{2,1,0:T(8,128)(2,1)S(1)}, bf16[16,296,128]{2,1,0:T(8,128)(2,1)S(1)}, u32[]{:S(2)}, u32[]{:S(2)}) %collective-permute-start.1) | collective-permute-done | bytes 1212448 | tf_op jit(solution)/shard_map/ppermute | solution.py:161
  36.9 0.0 copy-done
  36.9 9.9 %shard_map.75.begun = f32[17,296,128]{2,1,0:T(8,128)S(1)} custom-call(s32[256]{0:T(256)S(1)} %broadcast_add_fusion.items, s32[3]{0:T(128)S(1)} %and_select_fusion.ends, bf16[20,289,289]{2,1,0:T(8,128)(2,1)S(1)} %copy-done, bf16[16,296,128]{2,1,0:T(8,128)(2,1)S(1)} %all_to_all.10.panel.own_panel, bf16[16,296,128]{2,1,0:T(8,128)(2,1)S(1)} %collective-permute-done.1.other_panel), custom_call_target="tpu_custom_call" | custom-call | flops 21381376 | bytes 65536 | tf_op jit(solution)/shard_map/pallas_call | solution.py:176
  46.8 0.0 collective-permute-done.panel
  46.8 5.2 %shard_map.76 = s16[16,296,128]{2,1,0:T(8,128)(2,1)S(1)} custom-call(s32[256]{0:T(256)S(1)} %broadcast_add_fusion.items, s32[3]{0:T(128)S(1)} %and_select_fusion.ends, bf16[20,289,289]{2,1,0:T(8,128)(2,1)S(1)} %copy-done, bf16[16,296,128]{2,1,0:T(8,128)(2,1)S(1)} %collective-permute-done.panel, f32[17,296,128]{2,1,0:T(8,128)S(1)} %shard_map.75.begun), custom_call_target="tpu_custom_call" | custom-call | flops 4105224192 | bytes 8388608 | tf_op jit(solution)/shard_map/pallas_call | solution.py:184
  52.0 22.5 %all_to_all.11.moved = s16[16,296,128]{2,1,0:T(8,128)(2,1)S(1)} all-to-all(s16[16,296,128]{2,1,0:T(8,128)(2,1)S(1)} %shard_map.76), channel_id=1, replica_groups=mesh['grp'=32,'own'=16] {'own'}, dimensions={0} | all-to-all | bytes 2424832 | tf_op jit(solution)/shard_map/all_to_all | solution.py:193
  74.5 1.0 %shard_map.77 = f32[289,128]{1,0:T(8,128)} custom-call(s16[16,296,128]{2,1,0:T(8,128)(2,1)S(1)} %all_to_all.11.moved), custom_call_target="tpu_custom_call" | custom-call | tf_op jit(solution)/shard_map/pallas_call | solution.py:194
  (10 shorter events, 0.1 us)
Async XLA Ops:
  1.0 35.9 %copy-start = (bf16[20,289,289]{2,1,0:T(8,128)(2,1)S(1)}, bf16[20,289,289]{2,1,0:T(8,128)(2,1)}, u32[]{:S(2)}) copy-start(bf16[20,289,289]{2,1,0:T(8,128)(2,1)} %operators.3) | copy-start | bytes 10022524
  27.1 2.0 %copy-start.3 = (s32[192,1]{0,1:T(1,128)S(1)}, s32[192,1]{0,1:T(1,128)}, u32[]{:S(2)}) copy-start(s32[192,1]{0,1:T(1,128)} %param.9) | copy-start | bytes 2308
  27.1 2.0 %copy-start.4 = (s32[1,16]{1,0:T(1,128)S(1)}, s32[1,16]{1,0:T(1,128)}, u32[]{:S(2)}) copy-start(s32[1,16]{1,0:T(1,128)} %param.12) | copy-start | bytes 196
  27.1 2.1 %copy-start.1 = (s32[192]{0:T(256)S(1)}, s32[192]{0:T(256)}, u32[]{:S(2)}) copy-start(s32[192]{0:T(256)} %param.10) | copy-start | bytes 2308
  27.1 2.2 %copy-start.2 = (s32[192]{0:T(256)S(1)}, s32[192]{0:T(256)}, u32[]{:S(2)}) copy-start(s32[192]{0:T(256)} %param.11) | copy-start | bytes 2308
  27.1 7.8 %copy-start.5 = (s32[3]{0:T(128)S(1)}, s32[3]{0:T(128)}, u32[]{:S(2)}) copy-start(s32[3]{0:T(128)} %constant.71) | copy-start | bytes 40
  27.2 19.6 %collective-permute-start = (bf16[16,296,128]{2,1,0:T(8,128)(2,1)S(1)}, bf16[16,296,128]{2,1,0:T(8,128)(2,1)S(1)}, u32[]{:S(2)}, u32[]{:S(2)}) collective-permute-start(bf16[16,296,128]{2,1,0:T(8,128)(2,1)S(1)} %shard_map.74), channel_id=1, source_target_pairs={{16,32},{48,64},{80,96},{112,128},{144,160},{176,192},{208,224},{2... | collective-permute-start | bytes 3637256 | tf_op jit(solution)/shard_map/ppermute | solution.py:173
  29.2 7.6 %collective-permute-start.1 = (bf16[16,296,128]{2,1,0:T(8,128)(2,1)S(1)}, bf16[16,296,128]{2,1,0:T(8,128)(2,1)S(1)}, u32[]{:S(2)}, u32[]{:S(2)}) collective-permute-start(bf16[16,296,128]{2,1,0:T(8,128)(2,1)S(1)} %all_to_all.10.panel.own_panel), channel_id=1, source_target_pairs={{0,16},{16,0},{32,48},{48,32},{64,80},{80,64},{96,112},{112,96},{1... | collective-permute-start | bytes 3637256 | tf_op jit(solution)/shard_map/ppermute | solution.py:161
